TPU v7x, 128 devices: a whole 4x4x4 slice. The times are simulated.
128 devices in a mesh: gx: 4 (over y), gy: 4 (over z), gz: 8 (over x, core).
Axes of the slice: x: 4, y: 4, z: 4, core: 2. Of those that a mesh axis runs over, the one named last changes fastest.
Arguments:
- latent: bfloat16 [262144, 256], P(('gx', 'gy', 'gz')), may hold values from -6 to 6
- live_count: int32 [128], P(('gx', 'gy', 'gz')), may hold values from 640 to 2048, as said below
- leave_rows: int32 [16384], P(('gx', 'gy', 'gz')), may hold values from 0 to 2047, as said below
- leave_target: int32 [16384, 1], P(('gx', 'gy', 'gz')), may hold values from 0 to 127, as said below
- halo_rows: int32 [65536], P(('gx', 'gy', 'gz')), may hold values from 0 to 2303, as said below
- neighbours: int32 [294912, 24], P(('gx', 'gy', 'gz')), may hold values from -1 to 16127, as said below
- edge_in: bfloat16 [2, 2, 256, 256], replicated, may hold values from -0.25 to 0.25
- edge_bias: float32 [2, 256], replicated, may hold values from -3 to 3
- edge_out: bfloat16 [2, 256, 256], replicated, may hold values from -0.375 to 0.375
- edge_shift: float32 [2, 256], replicated, may hold values from -3 to 3
- edge_gain: float32 [2, 256], replicated, may hold values from 0.1 to 1.9
- node_in: bfloat16 [2, 2, 256, 256], replicated, may hold values from -0.25 to 0.25
- node_bias: float32 [2, 256], replicated, may hold values from -3 to 3
- node_out: bfloat16 [2, 256, 256], replicated, may hold values from -0.375 to 0.375
- node_shift: float32 [2, 256], replicated, may hold values from -3 to 3
- node_gain: float32 [2, 256], replicated, may hold values from 0.1 to 1.9
Outputs:
- updated: bfloat16 [294912, 256], P(('gx', 'gy', 'gz'))
Inputs may be any that keep to these rules, and one draw needn't show every extreme that they name: `live_count`: every domain has at least 640 live slots; some domain has all 2048. `leave_rows`: the 128 entries of a domain are distinct slots below its live_count. `leave_target`: A domain number; one source sends at most 2 rows to one domain, and every source sends exactly 2 rows to some domain. A target may be the source itself. `halo_rows`: the 512 entries of a domain are distinct rows of its table that hold a particle. `neighbours`: -1 marks an empty slot. Rows that hold no particle have only empty slots.
All inputs are finite; a program needn't handle non-finite values.
Results may differ from a plain program's by a relative error of at most 0.01.
Values may be sent and summed in bfloat16 or wider, within the bound.
A program may use at most 64 MiB of HBM per device.

v0:
```python
import jax
import jax.numpy as jnp
from jax import lax
from jax.sharding import PartitionSpec as P

eps = 1e-05


def with_halo(x, sides, width):
    for axis, dim in sides:
        devices, length = (lax.axis_size(axis), x.shape[dim])
        up = [(i, (i + 1) % devices) for i in range(devices - 1)]
        down = [(j, i) for i, j in up]
        last = lax.slice_in_dim(x, length - width, length, axis=dim)
        first = lax.slice_in_dim(x, 0, width, axis=dim)
        before = lax.ppermute(last, axis, up)
        after = lax.ppermute(first, axis, down)
        x = jnp.concatenate([before, x, after], axis=dim)
    return x


def layer_norm(values, feature_gain):
    average = jnp.mean(values, axis=-1, keepdims=True)
    centred = values - average
    spread = jnp.mean(centred * centred, axis=-1, keepdims=True)
    return centred * lax.rsqrt(spread + eps) * feature_gain


def message_rows(
    node_table,
    senders,
    neighbour_ids,
    living,
    receive_weight,
    edge_bias,
    edge_out,
    edge_shift,
    edge_gain,
    node_self,
    node_message,
    node_bias,
    node_out,
    node_shift,
    node_gain,
):
    table_rows = node_table.shape[0]
    slot_count = neighbour_ids.shape[1]
    receive = jnp.dot(node_table, receive_weight, preferred_element_type=jnp.float32)
    present = neighbour_ids >= 0
    picked = jnp.take(senders, jnp.where(present, neighbour_ids, 0), axis=0, mode="clip")
    edge_input = receive[:, None, :] + picked.astype(jnp.float32) + edge_bias
    active = jnp.maximum(edge_input, 0.0).astype(jnp.bfloat16).reshape(table_rows * slot_count, -1)
    edge_raw = jnp.dot(active, edge_out, preferred_element_type=jnp.float32) + edge_shift
    message = layer_norm(edge_raw, edge_gain).reshape(table_rows, slot_count, -1)
    summed = jnp.sum(message * present[:, :, None].astype(jnp.float32), axis=1).astype(jnp.bfloat16)
    hidden = (
        jnp.dot(node_table, node_self, preferred_element_type=jnp.float32)
        + jnp.dot(summed, node_message, preferred_element_type=jnp.float32)
        + node_bias
    )
    hidden = jnp.maximum(hidden, 0.0).astype(jnp.bfloat16)
    node_raw = jnp.dot(hidden, node_out, preferred_element_type=jnp.float32) + node_shift
    renewed = (node_table.astype(jnp.float32) + layer_norm(node_raw, node_gain)) * living[:, None]
    return renewed.astype(jnp.bfloat16)


def pick_rows(source_rows, row_ids):
    selector = (
        row_ids[:, None] == jnp.arange(source_rows.shape[0], dtype=jnp.int32)[None, :]
    ).astype(source_rows.dtype)
    return jnp.dot(selector, source_rows, preferred_element_type=jnp.float32).astype(
        source_rows.dtype
    )


def local(
    latent,
    live_count,
    leave_rows,
    leave_target,
    halo_rows,
    neighbours,
    edge_in,
    edge_bias,
    edge_out,
    edge_shift,
    edge_gain,
    node_in,
    node_bias,
    node_out,
    node_shift,
    node_gain,
):
    devices = lax.axis_size(("gx", "gy", "gz"))
    local_rows = latent.shape[0]
    feature_width = latent.shape[1]
    slots_total = neighbours.shape[0] - local_rows
    capacity = slots_total // devices
    leaving = leave_rows.shape[0]
    target_domain = leave_target[:, 0]
    order_rows = jnp.arange(leaving, dtype=jnp.int32)
    earlier = order_rows[None, :] < order_rows[:, None]
    same_target = target_domain[:, None] == target_domain[None, :]
    row_rank = jnp.sum(jnp.logical_and(same_target, earlier).astype(jnp.int32), axis=1)
    position = target_domain * capacity + row_rank
    moving = pick_rows(latent, leave_rows)
    placement = jnp.arange(slots_total, dtype=jnp.int32)[:, None] == position[None, :]
    outgoing = jnp.dot(
        placement.astype(jnp.bfloat16), moving, preferred_element_type=jnp.float32
    ).astype(jnp.bfloat16)
    filled = jnp.any(placement, axis=1).astype(jnp.bfloat16)
    arrived, arrival_flags = (
        lax.all_to_all(
            outgoing.reshape(devices, capacity, feature_width),
            ("gx", "gy", "gz"),
            split_axis=0,
            concat_axis=0,
            tiled=True,
        ),
        lax.all_to_all(
            filled.reshape(devices, capacity),
            ("gx", "gy", "gz"),
            split_axis=0,
            concat_axis=0,
            tiled=True,
        ),
    )
    node_table = jnp.concatenate([latent, arrived.reshape(slots_total, feature_width)], axis=0)
    local_index = jnp.arange(local_rows, dtype=jnp.int32)
    departed = jnp.any(local_index[:, None] == leave_rows[None, :], axis=1)
    local_live = jnp.where(
        jnp.logical_and(local_index < live_count[0], jnp.logical_not(departed)), 1.0, 0.0
    ).astype(jnp.float32)
    living = jnp.concatenate([local_live, arrival_flags.reshape(slots_total).astype(jnp.float32)])
    table_rows = node_table.shape[0]
    block_rows = 64
    for trial in (512, 256, 128):
        if table_rows % trial == 0 and block_rows == 64:
            block_rows = trial
    block_count = table_rows // block_rows
    slot_count = neighbours.shape[1]
    blocked_ids = neighbours.reshape(block_count, block_rows, slot_count)
    blocked_live = living.reshape(block_count, block_rows)
    for step_index in range(edge_in.shape[0]):
        send_weight = edge_in[step_index, 1]
        own_projection = jnp.dot(
            node_table, send_weight, preferred_element_type=jnp.float32
        ).astype(jnp.bfloat16)
        boundary = pick_rows(node_table, halo_rows)
        beside_all = with_halo(
            boundary.reshape(1, 1, 1, boundary.shape[0], feature_width),
            (("gx", 0), ("gy", 1), ("gz", 2)),
            1,
        )
        ghosts = jnp.dot(
            beside_all.reshape(-1, feature_width), send_weight, preferred_element_type=jnp.float32
        ).astype(jnp.bfloat16)
        senders = jnp.concatenate([own_projection, ghosts], axis=0)

        def one_block(pieces):
            own_rows, block_ids, block_live = pieces

            def compute(unused):
                return message_rows(
                    own_rows,
                    senders,
                    block_ids,
                    block_live,
                    edge_in[step_index, 0],
                    edge_bias[step_index],
                    edge_out[step_index],
                    edge_shift[step_index],
                    edge_gain[step_index],
                    node_in[step_index, 0],
                    node_in[step_index, 1],
                    node_bias[step_index],
                    node_out[step_index],
                    node_shift[step_index],
                    node_gain[step_index],
                )

            def vacant(unused):
                return jnp.zeros_like(own_rows)

            return lax.cond(jnp.any(block_live > 0.0), compute, vacant, 0)

        node_table = lax.map(
            one_block,
            (node_table.reshape(block_count, block_rows, feature_width), blocked_ids, blocked_live),
        ).reshape(table_rows, feature_width)
    return node_table


def solution(mesh):
    in_specs = (
        P(("gx", "gy", "gz"), None),
        P(("gx", "gy", "gz")),
        P(("gx", "gy", "gz")),
        P(("gx", "gy", "gz"), None),
        P(("gx", "gy", "gz")),
        P(("gx", "gy", "gz"), None),
        P(),
        P(),
        P(),
        P(),
        P(),
        P(),
        P(),
        P(),
        P(),
        P(),
    )
    out_specs = P(("gx", "gy", "gz"), None)
    return jax.shard_map(local, mesh=mesh, in_specs=in_specs, out_specs=out_specs, check_vma=False)
```

profile of v0, /device:TPU:12, one launch (start us, length us, event | category | flops | bytes accessed | tf_op | source)
XLA Modules:
  0.0 984.6 jit_solution(3642552606568219938)
XLA Ops:
  119.6 388.0 %while.20 = (s32[]{:T(128)}, bf16[9,256,256]{1,2,0:T(8,128)(2,1)}, f32[9,256]{1,0:T(8,128)}, bf16[9,256,256]{1,2,0:T(8,128)(2,1)}, bf16[2,2,256,256]{3,2,1,0:T(8...) while((s32[]{:T(128)}, bf16[9,256,256]{1,2,0:T(8,128)(2,1)}, ...), condition=%wide.region_12.13_spmd, body=%wide.region_3.12_spmd.sunk | while | flops 964137728 | bytes 55419784 | solution.py:187
  121.9 39.4 %conditional.4 = (bf16[1,256,256]{1,2,0:T(8,128)(2,1)}) conditional(s32[]{:T(128)} %convert_element_type.240, () %tuple.65, (bf16[9,256,256]{1,2,0:T(8,128)(2,1)}, s32[]{:T(128)}, bf16[2,2,256,256]{3,2,1,0:T(8,128)(2,1)}, bf16[2,2,256,256]{3,2,1,0:T(8,128)(2,1)}, s32[9,256,24]{2,1,0:T(8,128)}, /*index=5*/bf16[16128,256]{1,0:T(8,128)(2,1)}, ...), branch_computations={%region_5.5_spmd, %region_6.11_spmd} | conditional | flops 964137216 | bytes 55153768 | solution.py:185
  124.2 23.8 %gather_fusion = bf16[6144,256]{1,0:T(8,128)(2,1)S(1)} fusion(bf16[16128,256]{1,0:T(8,128)(2,1)} %get-tuple-element.347, s32[6144]{0:T(1024)S(1)} %broadcast_clamp_fusion), kind=kCustom, calls=%fused_computation | custom fusion | bytes 6316032 | tf_op jit(solution)/shard_map/while/body/eval_jaxpr/cond/branch_1_fun/jit(_take)/gather | solution.py:50
  165.0 39.4 %conditional.4 = (bf16[1,256,256]{1,2,0:T(8,128)(2,1)}) conditional(s32[]{:T(128)} %convert_element_type.240, () %tuple.65, (bf16[9,256,256]{1,2,0:T(8,128)(2,1)}, s32[]{:T(128)}, bf16[2,2,256,256]{3,2,1,0:T(8,128)(2,1)}, bf16[2,2,256,256]{3,2,1,0:T(8,128)(2,1)}, s32[9,256,24]{2,1,0:T(8,128)}, /*index=5*/bf16[16128,256]{1,0:T(8,128)(2,1)}, ...), branch_computations={%region_5.5_spmd, %region_6.11_spmd} | conditional | flops 964137216 | bytes 55153768 | solution.py:185
  167.3 23.8 %gather_fusion = bf16[6144,256]{1,0:T(8,128)(2,1)S(1)} fusion(bf16[16128,256]{1,0:T(8,128)(2,1)} %get-tuple-element.347, s32[6144]{0:T(1024)S(1)} %broadcast_clamp_fusion), kind=kCustom, calls=%fused_computation | custom fusion | bytes 6316032 | tf_op jit(solution)/shard_map/while/body/eval_jaxpr/cond/branch_1_fun/jit(_take)/gather | solution.py:50
  208.1 39.4 %conditional.4 = (bf16[1,256,256]{1,2,0:T(8,128)(2,1)}) conditional(s32[]{:T(128)} %convert_element_type.240, () %tuple.65, (bf16[9,256,256]{1,2,0:T(8,128)(2,1)}, s32[]{:T(128)}, bf16[2,2,256,256]{3,2,1,0:T(8,128)(2,1)}, bf16[2,2,256,256]{3,2,1,0:T(8,128)(2,1)}, s32[9,256,24]{2,1,0:T(8,128)}, /*index=5*/bf16[16128,256]{1,0:T(8,128)(2,1)}, ...), branch_computations={%region_5.5_spmd, %region_6.11_spmd} | conditional | flops 964137216 | bytes 55153768 | solution.py:185
  210.4 23.8 %gather_fusion = bf16[6144,256]{1,0:T(8,128)(2,1)S(1)} fusion(bf16[16128,256]{1,0:T(8,128)(2,1)} %get-tuple-element.347, s32[6144]{0:T(1024)S(1)} %broadcast_clamp_fusion), kind=kCustom, calls=%fused_computation | custom fusion | bytes 6316032 | tf_op jit(solution)/shard_map/while/body/eval_jaxpr/cond/branch_1_fun/jit(_take)/gather | solution.py:50
  251.2 39.4 %conditional.4 = (bf16[1,256,256]{1,2,0:T(8,128)(2,1)}) conditional(s32[]{:T(128)} %convert_element_type.240, () %tuple.65, (bf16[9,256,256]{1,2,0:T(8,128)(2,1)}, s32[]{:T(128)}, bf16[2,2,256,256]{3,2,1,0:T(8,128)(2,1)}, bf16[2,2,256,256]{3,2,1,0:T(8,128)(2,1)}, s32[9,256,24]{2,1,0:T(8,128)}, /*index=5*/bf16[16128,256]{1,0:T(8,128)(2,1)}, ...), branch_computations={%region_5.5_spmd, %region_6.11_spmd} | conditional | flops 964137216 | bytes 55153768 | solution.py:185
  253.5 23.8 %gather_fusion = bf16[6144,256]{1,0:T(8,128)(2,1)S(1)} fusion(bf16[16128,256]{1,0:T(8,128)(2,1)} %get-tuple-element.347, s32[6144]{0:T(1024)S(1)} %broadcast_clamp_fusion), kind=kCustom, calls=%fused_computation | custom fusion | bytes 6316032 | tf_op jit(solution)/shard_map/while/body/eval_jaxpr/cond/branch_1_fun/jit(_take)/gather | solution.py:50
  294.3 39.4 %conditional.4 = (bf16[1,256,256]{1,2,0:T(8,128)(2,1)}) conditional(s32[]{:T(128)} %convert_element_type.240, () %tuple.65, (bf16[9,256,256]{1,2,0:T(8,128)(2,1)}, s32[]{:T(128)}, bf16[2,2,256,256]{3,2,1,0:T(8,128)(2,1)}, bf16[2,2,256,256]{3,2,1,0:T(8,128)(2,1)}, s32[9,256,24]{2,1,0:T(8,128)}, /*index=5*/bf16[16128,256]{1,0:T(8,128)(2,1)}, ...), branch_computations={%region_5.5_spmd, %region_6.11_spmd} | conditional | flops 964137216 | bytes 55153768 | solution.py:185
  337.4 39.4 %conditional.4 = (bf16[1,256,256]{1,2,0:T(8,128)(2,1)}) conditional(s32[]{:T(128)} %convert_element_type.240, () %tuple.65, (bf16[9,256,256]{1,2,0:T(8,128)(2,1)}, s32[]{:T(128)}, bf16[2,2,256,256]{3,2,1,0:T(8,128)(2,1)}, bf16[2,2,256,256]{3,2,1,0:T(8,128)(2,1)}, s32[9,256,24]{2,1,0:T(8,128)}, /*index=5*/bf16[16128,256]{1,0:T(8,128)(2,1)}, ...), branch_computations={%region_5.5_spmd, %region_6.11_spmd} | conditional | flops 964137216 | bytes 55153768 | solution.py:185
  380.5 39.4 %conditional.4 = (bf16[1,256,256]{1,2,0:T(8,128)(2,1)}) conditional(s32[]{:T(128)} %convert_element_type.240, () %tuple.65, (bf16[9,256,256]{1,2,0:T(8,128)(2,1)}, s32[]{:T(128)}, bf16[2,2,256,256]{3,2,1,0:T(8,128)(2,1)}, bf16[2,2,256,256]{3,2,1,0:T(8,128)(2,1)}, s32[9,256,24]{2,1,0:T(8,128)}, /*index=5*/bf16[16128,256]{1,0:T(8,128)(2,1)}, ...), branch_computations={%region_5.5_spmd, %region_6.11_spmd} | conditional | flops 964137216 | bytes 55153768 | solution.py:185
  423.6 39.4 %conditional.4 = (bf16[1,256,256]{1,2,0:T(8,128)(2,1)}) conditional(s32[]{:T(128)} %convert_element_type.240, () %tuple.65, (bf16[9,256,256]{1,2,0:T(8,128)(2,1)}, s32[]{:T(128)}, bf16[2,2,256,256]{3,2,1,0:T(8,128)(2,1)}, bf16[2,2,256,256]{3,2,1,0:T(8,128)(2,1)}, s32[9,256,24]{2,1,0:T(8,128)}, /*index=5*/bf16[16128,256]{1,0:T(8,128)(2,1)}, ...), branch_computations={%region_5.5_spmd, %region_6.11_spmd} | conditional | flops 964137216 | bytes 55153768 | solution.py:185
  466.7 39.4 %conditional.4 = (bf16[1,256,256]{1,2,0:T(8,128)(2,1)}) conditional(s32[]{:T(128)} %convert_element_type.240, () %tuple.65, (bf16[9,256,256]{1,2,0:T(8,128)(2,1)}, s32[]{:T(128)}, bf16[2,2,256,256]{3,2,1,0:T(8,128)(2,1)}, bf16[2,2,256,256]{3,2,1,0:T(8,128)(2,1)}, s32[9,256,24]{2,1,0:T(8,128)}, /*index=5*/bf16[16128,256]{1,0:T(8,128)(2,1)}, ...), branch_computations={%region_5.5_spmd, %region_6.11_spmd} | conditional | flops 964137216 | bytes 55153768 | solution.py:185
  595.6 389.0 %while.21 = (s32[]{:T(128)}, bf16[9,256,256]{2,1,0:T(8,128)(2,1)}, f32[9,256]{1,0:T(8,128)}, bf16[9,256,256]{1,2,0:T(8,128)(2,1)}, bf16[2,2,256,256]{3,2,1,0:T(8...) while((s32[]{:T(128)}, bf16[9,256,256]{2,1,0:T(8,128)(2,1)}, ...), condition=%wide.region_22.23_spmd, body=%wide.region_13.22_spmd.sunk | while | flops 964137728 | bytes 55681928 | solution.py:187
  597.7 39.4 %conditional.5 = (bf16[1,256,256]{1,2,0:T(8,128)(2,1)}) conditional(s32[]{:T(128)} %convert_element_type.241, () %tuple.68, (bf16[9,256,256]{1,2,0:T(8,128)(2,1)}, s32[]{:T(128)}, bf16[2,2,256,256]{3,2,1,0:T(8,128)(2,1)}, bf16[2,2,256,256]{3,2,1,0:T(8,128)(2,1)}, s32[9,256,24]{2,1,0:T(8,128)}, /*index=5*/bf16[16128,256]{1,0:T(8,128)(2,1)}, ...), branch_computations={%region_15.15_spmd, %region_16.21_spmd} | conditional | flops 964137216 | bytes 55153768 | solution.py:185
  641.0 39.4 %conditional.5 = (bf16[1,256,256]{1,2,0:T(8,128)(2,1)}) conditional(s32[]{:T(128)} %convert_element_type.241, () %tuple.68, (bf16[9,256,256]{1,2,0:T(8,128)(2,1)}, s32[]{:T(128)}, bf16[2,2,256,256]{3,2,1,0:T(8,128)(2,1)}, bf16[2,2,256,256]{3,2,1,0:T(8,128)(2,1)}, s32[9,256,24]{2,1,0:T(8,128)}, /*index=5*/bf16[16128,256]{1,0:T(8,128)(2,1)}, ...), branch_computations={%region_15.15_spmd, %region_16.21_spmd} | conditional | flops 964137216 | bytes 55153768 | solution.py:185
  684.2 39.4 %conditional.5 = (bf16[1,256,256]{1,2,0:T(8,128)(2,1)}) conditional(s32[]{:T(128)} %convert_element_type.241, () %tuple.68, (bf16[9,256,256]{1,2,0:T(8,128)(2,1)}, s32[]{:T(128)}, bf16[2,2,256,256]{3,2,1,0:T(8,128)(2,1)}, bf16[2,2,256,256]{3,2,1,0:T(8,128)(2,1)}, s32[9,256,24]{2,1,0:T(8,128)}, /*index=5*/bf16[16128,256]{1,0:T(8,128)(2,1)}, ...), branch_computations={%region_15.15_spmd, %region_16.21_spmd} | conditional | flops 964137216 | bytes 55153768 | solution.py:185
  727.4 39.4 %conditional.5 = (bf16[1,256,256]{1,2,0:T(8,128)(2,1)}) conditional(s32[]{:T(128)} %convert_element_type.241, () %tuple.68, (bf16[9,256,256]{1,2,0:T(8,128)(2,1)}, s32[]{:T(128)}, bf16[2,2,256,256]{3,2,1,0:T(8,128)(2,1)}, bf16[2,2,256,256]{3,2,1,0:T(8,128)(2,1)}, s32[9,256,24]{2,1,0:T(8,128)}, /*index=5*/bf16[16128,256]{1,0:T(8,128)(2,1)}, ...), branch_computations={%region_15.15_spmd, %region_16.21_spmd} | conditional | flops 964137216 | bytes 55153768 | solution.py:185
  770.6 39.4 %conditional.5 = (bf16[1,256,256]{1,2,0:T(8,128)(2,1)}) conditional(s32[]{:T(128)} %convert_element_type.241, () %tuple.68, (bf16[9,256,256]{1,2,0:T(8,128)(2,1)}, s32[]{:T(128)}, bf16[2,2,256,256]{3,2,1,0:T(8,128)(2,1)}, bf16[2,2,256,256]{3,2,1,0:T(8,128)(2,1)}, s32[9,256,24]{2,1,0:T(8,128)}, /*index=5*/bf16[16128,256]{1,0:T(8,128)(2,1)}, ...), branch_computations={%region_15.15_spmd, %region_16.21_spmd} | conditional | flops 964137216 | bytes 55153768 | solution.py:185
  813.9 39.4 %conditional.5 = (bf16[1,256,256]{1,2,0:T(8,128)(2,1)}) conditional(s32[]{:T(128)} %convert_element_type.241, () %tuple.68, (bf16[9,256,256]{1,2,0:T(8,128)(2,1)}, s32[]{:T(128)}, bf16[2,2,256,256]{3,2,1,0:T(8,128)(2,1)}, bf16[2,2,256,256]{3,2,1,0:T(8,128)(2,1)}, s32[9,256,24]{2,1,0:T(8,128)}, /*index=5*/bf16[16128,256]{1,0:T(8,128)(2,1)}, ...), branch_computations={%region_15.15_spmd, %region_16.21_spmd} | conditional | flops 964137216 | bytes 55153768 | solution.py:185
  857.1 39.4 %conditional.5 = (bf16[1,256,256]{1,2,0:T(8,128)(2,1)}) conditional(s32[]{:T(128)} %convert_element_type.241, () %tuple.68, (bf16[9,256,256]{1,2,0:T(8,128)(2,1)}, s32[]{:T(128)}, bf16[2,2,256,256]{3,2,1,0:T(8,128)(2,1)}, bf16[2,2,256,256]{3,2,1,0:T(8,128)(2,1)}, s32[9,256,24]{2,1,0:T(8,128)}, /*index=5*/bf16[16128,256]{1,0:T(8,128)(2,1)}, ...), branch_computations={%region_15.15_spmd, %region_16.21_spmd} | conditional | flops 964137216 | bytes 55153768 | solution.py:185
  900.3 39.4 %conditional.5 = (bf16[1,256,256]{1,2,0:T(8,128)(2,1)}) conditional(s32[]{:T(128)} %convert_element_type.241, () %tuple.68, (bf16[9,256,256]{1,2,0:T(8,128)(2,1)}, s32[]{:T(128)}, bf16[2,2,256,256]{3,2,1,0:T(8,128)(2,1)}, bf16[2,2,256,256]{3,2,1,0:T(8,128)(2,1)}, s32[9,256,24]{2,1,0:T(8,128)}, /*index=5*/bf16[16128,256]{1,0:T(8,128)(2,1)}, ...), branch_computations={%region_15.15_spmd, %region_16.21_spmd} | conditional | flops 964137216 | bytes 55153768 | solution.py:185
  943.5 39.4 %conditional.5 = (bf16[1,256,256]{1,2,0:T(8,128)(2,1)}) conditional(s32[]{:T(128)} %convert_element_type.241, () %tuple.68, (bf16[9,256,256]{1,2,0:T(8,128)(2,1)}, s32[]{:T(128)}, bf16[2,2,256,256]{3,2,1,0:T(8,128)(2,1)}, bf16[2,2,256,256]{3,2,1,0:T(8,128)(2,1)}, s32[9,256,24]{2,1,0:T(8,128)}, /*index=5*/bf16[16128,256]{1,0:T(8,128)(2,1)}, ...), branch_computations={%region_15.15_spmd, %region_16.21_spmd} | conditional | flops 964137216 | bytes 55153768 | solution.py:185
  (700 shorter events, 872.2 us)
Async XLA Ops:
  4.1 17.7 %all-to-all-start.1 = ((bf16[128,2,256]{2,1,0:T(2,128)(2,1)}), bf16[128,2,256]{2,1,0:T(2,128)(2,1)S(1)}, u32[]{:S(2)}, u32[]{:S(2)}) async-start(bf16[128,2,256]{2,1,0:T(2,128)(2,1)} %reshape.252), calls=%async_computation.1 | async-start | bytes 262144 | tf_op jit(solution)/shard_map/all_to_all | solution.py:113
  23.5 52.2 %copy-start.14 = (s32[128]{0:T(128)S(1)}, s32[128]{0:T(128)}, u32[]{:S(2)}) copy-start(s32[128]{0:T(128)} %param.26) | copy-start | bytes 1540
  23.5 10.2 %collective-permute-start = (bf16[1,1,1,512,256]{4,3,2,1,0:T(8,128)(2,1)S(1)}, bf16[1,1,1,512,256]{4,3,2,1,0:T(8,128)(2,1)S(1)}, u32[]{:S(2)}, u32[]{:S(2)}) collective-permute-start(bf16[1,1,1,512,256]{4,3,2,1,0:T(8,128)(2,1)S(1)} %fusion.71), channel_id=1, source_target_pairs={{0,32},{32,64},{64,96},{1,33},{33,65},{65,97},{2,34},{34,66},{66,9... | collective-permute-start | bytes 786440 | tf_op jit(solution)/shard_map/ppermute | solution.py:16
  26.1 9.9 %collective-permute-start.1 = (bf16[1,1,1,512,256]{4,3,2,1,0:T(8,128)(2,1)S(1)}, bf16[1,1,1,512,256]{4,3,2,1,0:T(8,128)(2,1)S(1)}, u32[]{:S(2)}, u32[]{:S(2)}) collective-permute-start(bf16[1,1,1,512,256]{4,3,2,1,0:T(8,128)(2,1)S(1)} %fusion.71), channel_id=1, source_target_pairs={{32,0},{64,32},{96,64},{33,1},{65,33},{97,65},{34,2},{66,34},{98,6... | collective-permute-start | bytes 786440 | tf_op jit(solution)/shard_map/ppermute | solution.py:17
  36.1 18.7 %collective-permute-start.2 = (bf16[3,1,1,512,256]{4,3,2,1,0:T(8,128)(2,1)S(1)}, bf16[3,1,1,512,256]{4,3,2,1,0:T(8,128)(2,1)S(1)}, u32[]{:S(2)}, u32[]{:S(2)}) collective-permute-start(bf16[3,1,1,512,256]{4,3,2,1,0:T(8,128)(2,1)S(1)} %pad_maximum_fusion.6), channel_id=1, source_target_pairs={{0,8},{8,16},{16,24},{1,9},{9,17},{17,25},{2,10},{10,18},{18,26},{... | collective-permute-start | bytes 2359304 | tf_op jit(solution)/shard_map/ppermute | solution.py:16
  38.9 20.0 %collective-permute-start.3 = (bf16[3,1,1,512,256]{4,3,2,1,0:T(8,128)(2,1)S(1)}, bf16[3,1,1,512,256]{4,3,2,1,0:T(8,128)(2,1)S(1)}, u32[]{:S(2)}, u32[]{:S(2)}) collective-permute-start(bf16[3,1,1,512,256]{4,3,2,1,0:T(8,128)(2,1)S(1)} %pad_maximum_fusion.6), channel_id=1, source_target_pairs={{8,0},{16,8},{24,16},{9,1},{17,9},{25,17},{10,2},{18,10},{26,18},{... | collective-permute-start | bytes 2359304 | tf_op jit(solution)/shard_map/ppermute | solution.py:17
  60.5 42.8 %collective-permute-start.4 = (bf16[3,3,1,512,256]{4,3,2,1,0:T(8,128)(2,1)}, bf16[3,3,1,512,256]{4,3,2,1,0:T(8,128)(2,1)}, u32[]{:S(2)}, u32[]{:S(2)}) collective-permute-start(bf16[3,3,1,512,256]{4,3,2,1,0:T(8,128)(2,1)} %pad_maximum_fusion.4), channel_id=1, source_target_pairs={{0,1},{1,2},{2,3},{3,4},{4,5},{5,6},{6,7},{8,9},{9,10},{10,11},{11... | collective-permute-start | bytes 7077896 | tf_op jit(solution)/shard_map/ppermute | solution.py:16
  62.5 40.9 %collective-permute-start.5 = (bf16[3,3,1,512,256]{4,3,2,1,0:T(8,128)(2,1)}, bf16[3,3,1,512,256]{4,3,2,1,0:T(8,128)(2,1)}, u32[]{:S(2)}, u32[]{:S(2)}) collective-permute-start(bf16[3,3,1,512,256]{4,3,2,1,0:T(8,128)(2,1)} %pad_maximum_fusion.4), channel_id=1, source_target_pairs={{1,0},{2,1},{3,2},{4,3},{5,4},{6,5},{7,6},{9,8},{10,9},{11,10},{12... | collective-permute-start | bytes 7077896 | tf_op jit(solution)/shard_map/ppermute | solution.py:17
  67.0 29.5 %all-to-all-start = ((bf16[128,1,2]{2,1,0:T(2,128)(2,1)}), bf16[128,1,2]{2,1,0:T(2,128)(2,1)}, u32[]{:S(2)}, u32[]{:S(2)}) async-start(bf16[128,1,2]{2,1,0:T(2,128)(2,1)} %reshape.286), calls=%async_computation | async-start | bytes 131072 | tf_op jit(solution)/shard_map/all_to_all | solution.py:120
  109.7 9.8 %copy-start.6 = (f32[2,256]{1,0:T(2,128)S(1)}, f32[2,256]{1,0:T(2,128)}, u32[]{:S(2)}) copy-start(f32[2,256]{1,0:T(2,128)} %param.31) | copy-start | bytes 6148
  109.7 9.8 copy-start.7
  109.7 9.8 copy-start.8
  109.7 9.8 copy-start.9
  109.8 9.8 copy-start.10
  109.8 9.8 copy-start.12
  119.6 389.6 %copy-start.15 = (s32[512]{0:T(512)S(1)}, s32[512]{0:T(512)}, u32[]{:S(2)}) copy-start(s32[512]{0:T(512)} %param.28) | copy-start | bytes 6148
  510.2 9.3 collective-permute-start.6
  512.1 10.9 %collective-permute-start.7 = (bf16[1,1,1,512,256]{4,3,2,1,0:T(8,128)(2,1)S(1)}, bf16[1,1,1,512,256]{4,3,2,1,0:T(8,128)(2,1)S(1)}, u32[]{:S(2)}, u32[]{:S(2)}) collective-permute-start(bf16[1,1,1,512,256]{4,3,2,1,0:T(8,128)(2,1)S(1)} %fusion.70), channel_id=1, source_target_pairs={{32,0},{64,32},{96,64},{33,1},{65,33},{97,65},{34,2},{66,34},{98,6... | collective-permute-start | bytes 786440 | tf_op jit(solution)/shard_map/ppermute | solution.py:17
  523.1 18.5 %collective-permute-start.8 = (bf16[3,1,1,512,256]{4,3,2,1,0:T(8,128)(2,1)S(1)}, bf16[3,1,1,512,256]{4,3,2,1,0:T(8,128)(2,1)S(1)}, u32[]{:S(2)}, u32[]{:S(2)}) collective-permute-start(bf16[3,1,1,512,256]{4,3,2,1,0:T(8,128)(2,1)S(1)} %pad_maximum_fusion.7), channel_id=1, source_target_pairs={{0,8},{8,16},{16,24},{1,9},{9,17},{17,25},{2,10},{10,18},{18,26},{... | collective-permute-start | bytes 2359304 | tf_op jit(solution)/shard_map/ppermute | solution.py:16
  524.7 21.0 %collective-permute-start.9 = (bf16[3,1,1,512,256]{4,3,2,1,0:T(8,128)(2,1)S(1)}, bf16[3,1,1,512,256]{4,3,2,1,0:T(8,128)(2,1)S(1)}, u32[]{:S(2)}, u32[]{:S(2)}) collective-permute-start(bf16[3,1,1,512,256]{4,3,2,1,0:T(8,128)(2,1)S(1)} %pad_maximum_fusion.7), channel_id=1, source_target_pairs={{8,0},{16,8},{24,16},{9,1},{17,9},{25,17},{10,2},{18,10},{26,18},{... | collective-permute-start | bytes 2359304 | tf_op jit(solution)/shard_map/ppermute | solution.py:17
  547.3 30.5 %collective-permute-start.10 = (bf16[3,3,1,512,256]{4,3,2,1,0:T(8,128)(2,1)}, bf16[3,3,1,512,256]{4,3,2,1,0:T(8,128)(2,1)}, u32[]{:S(2)}, u32[]{:S(2)}) collective-permute-start(bf16[3,3,1,512,256]{4,3,2,1,0:T(8,128)(2,1)} %pad_maximum_fusion.5), channel_id=1, source_target_pairs={{0,1},{1,2},{2,3},{3,4},{4,5},{5,6},{6,7},{8,9},{9,10},{10,11},{11... | collective-permute-start | bytes 7077896 | tf_op jit(solution)/shard_map/ppermute | solution.py:16
  549.2 30.3 %collective-permute-start.11 = (bf16[3,3,1,512,256]{4,3,2,1,0:T(8,128)(2,1)}, bf16[3,3,1,512,256]{4,3,2,1,0:T(8,128)(2,1)}, u32[]{:S(2)}, u32[]{:S(2)}) collective-permute-start(bf16[3,3,1,512,256]{4,3,2,1,0:T(8,128)(2,1)} %pad_maximum_fusion.5), channel_id=1, source_target_pairs={{1,0},{2,1},{3,2},{4,3},{5,4},{6,5},{7,6},{9,8},{10,9},{11,10},{12... | collective-permute-start | bytes 7077896 | tf_op jit(solution)/shard_map/ppermute | solution.py:17
  585.8 9.8 copy-start.11
  585.8 9.8 copy-start.13
  (54 other events, 133.1 us)
where the time goes:
time: 989 us; the launch traced here: 985 us
  local copies, waits for them, and re-layouts  482 us (49%)
  other arithmetic  255 us (26%)
  waiting for transfers between devices  101 us (10%)
  matrix products  81.6 us (8%)
  starting transfers between devices  48.2 us (5%)
  loops' own time  16.4 us (2%)
    gather x18, local copies, waits for them, and re-layouts, message_rows(): jnp.take(senders, jnp.where(present, neighbour_ids, 0), axis=0, mode='clip')  428 us
    ppermute x6, waiting for transfers between devices, with_halo(): before = lax.ppermute(last, axis, up)  61.5 us
    mul x18, other arithmetic, layer_norm(): return centred * lax.rsqrt(spread + eps) * feature_gain  59.8 us
    reduce_sum x36, other arithmetic, layer_norm(): spread = jnp.mean(centred * centred, axis=-1, keepdims=True)  34.8 us
    broadcast_in_dim x18, other arithmetic, local(): lax.map(one_block, (node_table.reshape(block_count, block_rows, feature_w...  30.2 us
    dynamic_update_slice x27, local copies, waits for them, and re-layouts, local(): lax.map(one_block, (node_table.reshape(block_count, block_rows, feature_w...  29.1 us
    reduce_sum x18, other arithmetic, message_rows(): jnp.sum(message * present[:, :, None].astype(jnp.float32), axis=1)  27.3 us
    dot_general x18, matrix products, message_rows(): jnp.dot(node_table, receive_weight, preferred_element_type=jnp.float32)  21.5 us
  transfers between devices with their start and end apart: 14, of which 12 were waited for; matrix products, arithmetic and copies ran while one was open for 1% of the time, Pallas kernels for 0%

commit v1 on v0

v1 whole, which is shorter than its diff:
```python
import functools

import jax
import jax.numpy as jnp
from jax import lax
from jax.experimental import pallas as pl
from jax.experimental.pallas import tpu as pltpu
from jax.sharding import PartitionSpec as P

EPS = 1e-05
F32 = jnp.float32
BF16 = jnp.bfloat16
HALF = 128
ROWS = 32
CHUNK = 256
GROUP = 8
NODE_ROWS = 256
VMEM_BYTES = 56 * 2**20


def layer_norm(values, feature_gain):
    average = jnp.mean(values, axis=-1, keepdims=True)
    centred = values - average
    spread = jnp.mean(centred * centred, axis=-1, keepdims=True)
    return centred * lax.rsqrt(spread + EPS) * feature_gain


def store_split(pairs, first_row, values):
    count = values.shape[0]
    pairs[pl.ds(2 * first_row, count, stride=2), :] = values[:, :HALF]
    pairs[pl.ds(2 * first_row + 1, count, stride=2), :] = values[:, HALF:]


def project_rows(pairs, first_row, rows, weight):
    projected = jnp.dot(rows, weight, preferred_element_type=F32).astype(BF16)
    store_split(pairs, first_row, projected.astype(F32))
    return projected


def pick_boundary(pairs, halo_ids, picked, boundary_ref):
    count = boundary_ref.shape[0]

    @pl.loop(0, count // 64)
    def _(block):
        for g in range(64 // GROUP):
            ids = halo_ids.at[pl.ds(block * 64 + g * GROUP, GROUP)]
            for e in range(GROUP):
                row = pl.multiple_of(ids[e], 2)
                picked[pl.ds(2 * (g * GROUP + e), 2), :] = pairs[pl.ds(row, 2), :]
        here = pl.ds(pl.multiple_of(block * 64, 64), 64)
        boundary_ref[here, :HALF] = picked[pl.ds(0, 64, stride=2), :].astype(BF16)
        boundary_ref[here, HALF:] = picked[pl.ds(1, 64, stride=2), :].astype(BF16)


def open_kernel(latent_ref, arrived_ref, halo_ids, weight_ref, table_ref, projected_ref, boundary_ref, pairs, picked):
    local_rows = latent_ref.shape[0]
    arrivals = arrived_ref.shape[0]

    @pl.loop(0, local_rows // NODE_ROWS)
    def _(i):
        first = pl.multiple_of(i * NODE_ROWS, NODE_ROWS)
        rows = latent_ref[pl.ds(first, NODE_ROWS), :]
        table_ref[pl.ds(first, NODE_ROWS), :] = rows
        projected_ref[pl.ds(first, NODE_ROWS), :] = project_rows(pairs, first, rows, weight_ref[...])

    rows = arrived_ref[...]
    table_ref[pl.ds(local_rows, arrivals), :] = rows
    projected_ref[pl.ds(local_rows, arrivals), :] = project_rows(pairs, local_rows, rows, weight_ref[...])
    pick_boundary(pairs, halo_ids, picked, boundary_ref)


def open_table(latent, arrived, halo_ids, weight):
    rows = latent.shape[0] + arrived.shape[0]
    width = latent.shape[1]
    count = halo_ids.shape[0]
    vmem = pl.BlockSpec(memory_space=pltpu.VMEM)
    return pl.pallas_call(
        open_kernel,
        out_shape=(
            jax.ShapeDtypeStruct((rows, width), BF16),
            jax.ShapeDtypeStruct((rows, width), BF16),
            jax.ShapeDtypeStruct((count, width), BF16),
        ),
        in_specs=[vmem, vmem, pl.BlockSpec(memory_space=pltpu.SMEM), vmem],
        out_specs=(vmem, vmem, vmem),
        scratch_shapes=[pltpu.VMEM((2 * rows, HALF), F32), pltpu.VMEM((2 * 64, HALF), F32)],
        compiler_params=pltpu.CompilerParams(vmem_limit_bytes=VMEM_BYTES),
        name="open_table",
    )(latent, arrived, halo_ids, weight)


def step_kernel(slots, last, *refs):
    (
        block_total,
        edge_ids,
        ghosts,
        table_ref,
        projected_ref,
        floor_ref,
        living_ref,
        receive_weight,
        edge_bias,
        edge_out,
        edge_shift,
        edge_gain,
        node_self,
        node_message,
        node_bias,
        node_out,
        node_shift,
        node_gain,
    ) = refs[:18]
    if last:
        (renewed_ref,) = refs[18:19]
        rest = refs[19:]
    else:
        halo_ids, next_weight, renewed_ref, next_projected, boundary_ref = refs[18:23]
        rest = refs[23:]
    pairs, even, odd, receive, summed, raw, square, weight, staged, picked, sems = rest
    rows = table_ref.shape[0]
    width = table_ref.shape[1]
    edges = slots * ROWS
    blocks = rows // ROWS
    gathered = (even, odd)
    ghost_blocks, ghost_rows = ghosts.shape[0], ghosts.shape[1]

    def fetch(block, slot):
        return pltpu.make_async_copy(ghosts.at[block], staged.at[slot], sems.at[slot])

    fetch(0, 0).start()

    @pl.loop(0, rows // NODE_ROWS)
    def _(i):
        first = pl.multiple_of(i * NODE_ROWS, NODE_ROWS)
        here = pl.ds(first, NODE_ROWS)
        store_split(pairs, first, projected_ref[here, :].astype(F32))
        receive[here, :] = (
            jnp.dot(table_ref[here, :], receive_weight[...], preferred_element_type=F32) + edge_bias[...]
        )

    wide = edge_out[...].astype(F32)
    weight[...] = (wide - jnp.mean(wide, axis=1, keepdims=True)).astype(BF16)
    shift = edge_shift[...] - jnp.mean(edge_shift[...], axis=1, keepdims=True)

    @pl.loop(0, ghost_blocks)
    def _(block):
        slot = lax.rem(block, 2)
        fetch(block, slot).wait()

        @pl.when(block + 1 < ghost_blocks)
        def _():
            fetch(block + 1, 1 - slot).start()

        for piece in range(ghost_rows // NODE_ROWS):
            values = staged[slot, pl.ds(piece * NODE_ROWS, NODE_ROWS), :].astype(F32)
            store_split(pairs, pl.multiple_of(rows + block * ghost_rows + piece * NODE_ROWS, NODE_ROWS), values)

    def gather(into, block, start, stop):
        base = pl.multiple_of(block * edges, HALF)
        for e in range(start, stop):
            if e % GROUP == 0:
                ids = edge_ids.at[pl.ds(base + e, GROUP)]
            row = pl.multiple_of(ids[e % GROUP], 2)
            into[pl.ds(2 * e, 2), :] = pairs[pl.ds(row, 2), :]

    per_chunk = CHUNK // ROWS

    def first_half(source, first, chunk):
        own = receive[pl.ds(first, ROWS), :]
        left = source[pl.ds(2 * chunk * CHUNK, CHUNK, stride=2), :].reshape(per_chunk, ROWS, HALF)
        right = source[pl.ds(2 * chunk * CHUNK + 1, CHUNK, stride=2), :].reshape(per_chunk, ROWS, HALF)
        left = jnp.maximum(left + own[:, :HALF][None], 0.0).reshape(CHUNK, HALF).astype(BF16)
        right = jnp.maximum(right + own[:, HALF:][None], 0.0).reshape(CHUNK, HALF).astype(BF16)
        active = jnp.concatenate([left, right], axis=1)
        centred = jnp.dot(active, weight[...], preferred_element_type=F32) + shift
        total = jnp.sum(
            centred[:, :HALF] * centred[:, :HALF] + centred[:, HALF:] * centred[:, HALF:], axis=1, keepdims=True
        )
        here = pl.ds(chunk * CHUNK, CHUNK)
        raw[here, :] = centred
        square[here, :] = jnp.broadcast_to(total, (CHUNK, HALF))

    def second_half(floor, chunk, sums):
        left, right = sums
        for k in range(chunk * per_chunk, (chunk + 1) * per_chunk):
            here = pl.ds(k * ROWS, ROWS)
            scale = lax.rsqrt(square[here, :] * (1.0 / width) + floor[:, k : k + 1])
            left = left + raw[here, :HALF] * scale
            right = right + raw[here, HALF:] * scale
        return left, right

    chunks = edges // CHUNK
    gather(even, 0, 0, edges)

    @pl.loop(0, blocks // 2)
    def _(pair):
        for parity in range(2):
            block = 2 * pair + parity

            @pl.when(block < block_total[0])
            def _():
                first = pl.multiple_of(block * ROWS, ROWS)
                following = jnp.minimum(block + 1, blocks - 1)
                floor = floor_ref[pl.ds(first, ROWS), :]
                sums = (jnp.zeros((ROWS, HALF), F32), jnp.zeros((ROWS, HALF), F32))
                for chunk in range(chunks + 1):
                    if chunk < chunks:
                        gather(gathered[1 - parity], following, chunk * CHUNK, (chunk + 1) * CHUNK)
                        first_half(gathered[parity], first, chunk)
                    if chunk > 0:
                        sums = second_half(floor, chunk - 1, sums)
                summed[pl.ds(first, ROWS), :HALF] = sums[0]
                summed[pl.ds(first, ROWS), HALF:] = sums[1]

    @pl.loop(0, rows // NODE_ROWS)
    def _(i):
        first = pl.multiple_of(i * NODE_ROWS, NODE_ROWS)
        here = pl.ds(first, NODE_ROWS)
        own = table_ref[here, :]
        message = (summed[here, :] * edge_gain[...]).astype(BF16)
        hidden = (
            jnp.dot(own, node_self[...], preferred_element_type=F32)
            + jnp.dot(message, node_message[...], preferred_element_type=F32)
            + node_bias[...]
        )
        hidden = jnp.maximum(hidden, 0.0).astype(BF16)
        node_raw = jnp.dot(hidden, node_out[...], preferred_element_type=F32) + node_shift[...]
        renewed = (own.astype(F32) + layer_norm(node_raw, node_gain[...])) * living_ref[here, :]
        renewed = renewed.astype(BF16)
        renewed_ref[here, :] = renewed
        if not last:
            next_projected[here, :] = project_rows(pairs, first, renewed, next_weight[...])

    if not last:
        pick_boundary(pairs, halo_ids, picked, boundary_ref)


def message_step(block_total, edge_ids, ghosts, table, projected, floor, living, weights, halo_ids=None, next_weight=None):
    last = halo_ids is None
    rows, width = table.shape
    slots = floor.shape[1]
    edges = slots * ROWS
    ghost_total = ghosts.shape[0] * ghosts.shape[1]
    vmem = pl.BlockSpec(memory_space=pltpu.VMEM)
    smem = pl.BlockSpec(memory_space=pltpu.SMEM)
    out_shape = [jax.ShapeDtypeStruct((rows, width), BF16)]
    extra, extra_specs = [], []
    if not last:
        count = halo_ids.shape[0]
        out_shape += [jax.ShapeDtypeStruct((rows, width), BF16), jax.ShapeDtypeStruct((count, width), BF16)]
        extra, extra_specs = [halo_ids, next_weight], [smem, vmem]
    return pl.pallas_call(
        functools.partial(step_kernel, slots, last),
        out_shape=tuple(out_shape),
        in_specs=[smem, smem, pl.BlockSpec(memory_space=pl.ANY)] + [vmem] * (4 + len(weights)) + extra_specs,
        out_specs=tuple([vmem] * len(out_shape)),
        scratch_shapes=[
            pltpu.VMEM((2 * (rows + ghost_total), HALF), F32),
            pltpu.VMEM((2 * edges, HALF), F32),
            pltpu.VMEM((2 * edges, HALF), F32),
            pltpu.VMEM((rows, width), F32),
            pltpu.VMEM((rows, width), F32),
            pltpu.VMEM((edges, width), F32),
            pltpu.VMEM((edges, HALF), F32),
            pltpu.VMEM((width, width), BF16),
            pltpu.VMEM((2, ghosts.shape[1], width), BF16),
            pltpu.VMEM((2 * 64, HALF), F32),
            pltpu.SemaphoreType.DMA((2,)),
        ],
        compiler_params=pltpu.CompilerParams(vmem_limit_bytes=VMEM_BYTES),
        name="message_step",
    )(block_total, edge_ids, ghosts, table, projected, floor, living, *weights, *extra)


def with_halo(x, sides, width):
    for axis, dim in sides:
        devices, length = (lax.axis_size(axis), x.shape[dim])
        up = [(i, i + 1) for i in range(devices - 1)]
        down = [(j, i) for i, j in up]
        last = lax.slice_in_dim(x, length - width, length, axis=dim)
        first = lax.slice_in_dim(x, 0, width, axis=dim)
        before = lax.ppermute(last, axis, up)
        after = lax.ppermute(first, axis, down)
        x = jnp.concatenate([before, x, after], axis=dim)
    return x


def exchange(boundary):
    count, width = boundary.shape
    spread = with_halo(boundary.reshape(1, 1, 1, count, width), (("gx", 0), ("gy", 1), ("gz", 2)), 1)
    return spread.reshape(-1, count, width)


def pick_rows(source_rows, row_ids):
    selector = (
        row_ids[:, None] == jnp.arange(source_rows.shape[0], dtype=jnp.int32)[None, :]
    ).astype(source_rows.dtype)
    return jnp.dot(selector, source_rows, preferred_element_type=F32).astype(source_rows.dtype)


def local(
    latent,
    live_count,
    leave_rows,
    leave_target,
    halo_rows,
    neighbours,
    edge_in,
    edge_bias,
    edge_out,
    edge_shift,
    edge_gain,
    node_in,
    node_bias,
    node_out,
    node_shift,
    node_gain,
):
    axes = ("gx", "gy", "gz")
    devices = lax.axis_size(axes)
    local_rows, width = latent.shape
    table_rows, slots = neighbours.shape
    slots_total = table_rows - local_rows
    capacity = slots_total // devices
    leaving = leave_rows.shape[0]
    target_domain = leave_target[:, 0]
    order_rows = jnp.arange(leaving, dtype=jnp.int32)
    earlier = order_rows[None, :] < order_rows[:, None]
    same_target = target_domain[:, None] == target_domain[None, :]
    row_rank = jnp.sum(jnp.logical_and(same_target, earlier).astype(jnp.int32), axis=1)
    position = target_domain * capacity + row_rank
    moving = pick_rows(latent, leave_rows)
    moving = jnp.concatenate([moving, jnp.ones((leaving, HALF), BF16)], axis=1)
    placement = jnp.arange(slots_total, dtype=jnp.int32)[:, None] == position[None, :]
    outgoing = jnp.dot(placement.astype(BF16), moving, preferred_element_type=F32).astype(BF16)
    arrived = lax.all_to_all(
        outgoing.reshape(devices, capacity, width + HALF), axes, split_axis=0, concat_axis=0, tiled=True
    ).reshape(slots_total, width + HALF)
    local_index = jnp.arange(local_rows, dtype=jnp.int32)
    departed = jnp.any(local_index[:, None] == leave_rows[None, :], axis=1)
    local_live = jnp.logical_and(local_index < live_count[0], jnp.logical_not(departed)).astype(F32)
    living = jnp.concatenate([local_live[:, None], arrived[:, width : width + 1].astype(F32)], axis=0)

    blocks = table_rows // ROWS
    edge_ids = 2 * jnp.maximum(neighbours, 0)
    edge_ids = edge_ids.reshape(blocks, ROWS, slots).transpose(0, 2, 1).reshape(-1)
    floor = jnp.where(neighbours >= 0, EPS, jnp.inf).astype(F32)
    block_total = jnp.full((1,), blocks, jnp.int32)
    halo_ids = 2 * halo_rows

    table, projected, boundary = open_table(latent, arrived[:, :width], halo_ids, edge_in[0, 1])
    steps = edge_in.shape[0]
    for t in range(steps):
        ghosts = exchange(boundary)
        weights = (
            edge_in[t, 0],
            edge_bias[t][None],
            edge_out[t],
            edge_shift[t][None],
            edge_gain[t][None],
            node_in[t, 0],
            node_in[t, 1],
            node_bias[t][None],
            node_out[t],
            node_shift[t][None],
            node_gain[t][None],
        )
        if t < steps - 1:
            table, projected, boundary = message_step(
                block_total, edge_ids, ghosts, table, projected, floor, living, weights, halo_ids, edge_in[t + 1, 1]
            )
        else:
            (table,) = message_step(block_total, edge_ids, ghosts, table, projected, floor, living, weights)
    return table


def solution(mesh):
    rows = P(("gx", "gy", "gz"))
    in_specs = (rows,) * 6 + (P(),) * 10
    return jax.shard_map(local, mesh=mesh, in_specs=in_specs, out_specs=rows, check_vma=False)
```

time: 989 us -> 355 us (0.36)
  the two profiles are of different devices: /device:TPU:12 before, /device:TPU:18 now
where the time goes in v1:
time: 355 us; the launch traced here: 348 us
  Pallas kernels  171 us (48%)
  waiting for transfers between devices  102 us (29%)
  starting transfers between devices  42 us (12%)
  other arithmetic  22.2 us (6%)
  local copies, waits for them, and re-layouts  7.96 us (2%)
    pallas_call x2, Pallas kernels, message_step(): pl.pallas_call(functools.partial(step_kernel, slots, last), out_shape=tup...  166 us
    ppermute x6, waiting for transfers between devices, with_halo(): before = lax.ppermute(last, axis, up)  79.2 us
    ppermute x6, waiting for transfers between devices, with_halo(): after = lax.ppermute(first, axis, down)  16.7 us
    ppermute x6, starting transfers between devices, with_halo(): after = lax.ppermute(first, axis, down)  16.5 us
    concatenate x6, other arithmetic, with_halo(): x = jnp.concatenate([before, x, after], axis=dim)  16.1 us
    ppermute x6, starting transfers between devices, with_halo(): before = lax.ppermute(last, axis, up)  15.2 us
    all_to_all x1, starting transfers between devices, local(): lax.all_to_all(outgoing.reshape(devices, capacity, width + HALF), axes, s...  10.3 us
  transfers between devices with their start and end apart: 13, of which 13 were waited for; matrix products, arithmetic and copies ran while one was open for 3% of the time, Pallas kernels for 0%

profile of v1, /device:TPU:18, one launch (start us, length us, event | category | flops | bytes accessed | tf_op | source)
XLA Modules:
  0.0 348.3 jit_solution(11692065097881296679)
XLA Ops:
  4.2 10.3 %all-to-all-start = ((bf16[128,2,384]{2,1,0:T(2,128)(2,1)}), bf16[128,2,384]{2,1,0:T(2,128)(2,1)S(1)}, u32[]{:S(2)}, u32[]{:S(2)}) async-start(bf16[128,2,384]{2,1,0:T(2,128)(2,1)} %reshape.58), calls=%async_computation | async-start | bytes 393216 | tf_op jit(solution)/shard_map/all_to_all | solution.py:336
  16.1 6.2 %all-to-all-done = bf16[128,2,384]{2,1,0:T(2,128)(2,1)S(1)} async-done(((bf16[128,2,384]{2,1,0:T(2,128)(2,1)}), bf16[128,2,384]{2,1,0:T(2,128)(2,1)S(1)}, u32[]{:S(2)}, u32[]{:S(2)}) %all-to-all-start) | async-done | bytes 196640 | tf_op jit(solution)/shard_map/all_to_all | solution.py:336
  23.1 4.9 %open_table.1 = (bf16[2304,256]{1,0:T(8,128)(2,1)}, bf16[2304,256]{1,0:T(8,128)(2,1)}, bf16[512,256]{1,0:T(8,128)(2,1)}) custom-call(bf16[2048,256]{1,0:T(8,128)(2,1)} %latent_ref.1, bf16[256,256]{1,0:T(8,128)(2,1)} %slice.104.arrived_ref, s32[512]{0:T(512)} %broadcast_multiply_fusion.halo_ids.refs_18_, bf16[256,256]{1,0:T(8,128)(2,1)} %get-tuple-element.44.weight_ref), custom_call_target="tpu_custom_call" | custom-call | tf_op jit(solution)/shard_map/open_table/pallas_call | solution.py:77
  28.0 3.1 collective-permute-start
  31.1 2.8 collective-permute-start.1
  34.0 4.6 %collective-permute-done = bf16[1,1,1,512,256]{4,3,2,1,0:T(8,128)(2,1)S(1)} collective-permute-done((bf16[1,1,1,512,256]{4,3,2,1,0:T(8,128)(2,1)}, bf16[1,1,1,512,256]{4,3,2,1,0:T(8,128)(2,1)S(1)}, u32[]{:S(2)}, u32[]{:S(2)}) %collective-permute-start) | collective-permute-done | bytes 262176 | tf_op jit(solution)/shard_map/ppermute | solution.py:282
  38.5 2.7 collective-permute-done.1
  43.3 2.4 collective-permute-start.2
  48.2 13.7 %collective-permute-done.2 = bf16[3,1,1,512,256]{4,3,2,1,0:T(8,128)(2,1)S(1)} collective-permute-done((bf16[3,1,1,512,256]{4,3,2,1,0:T(8,128)(2,1)}, bf16[3,1,1,512,256]{4,3,2,1,0:T(8,128)(2,1)S(1)}, u32[]{:S(2)}, u32[]{:S(2)}) %collective-permute-start.2) | collective-permute-done | bytes 786464 | tf_op jit(solution)/shard_map/ppermute | solution.py:282
  61.9 4.2 %collective-permute-done.3 = bf16[3,1,1,512,256]{4,3,2,1,0:T(8,128)(2,1)} collective-permute-done((bf16[3,1,1,512,256]{4,3,2,1,0:T(8,128)(2,1)}, bf16[3,1,1,512,256]{4,3,2,1,0:T(8,128)(2,1)}, u32[]{:S(2)}, u32[]{:S(2)}) %collective-permute-start.3) | collective-permute-done | bytes 786464 | tf_op jit(solution)/shard_map/ppermute | solution.py:283
  66.0 2.5 pad_maximum_fusion.2
  70.7 3.6 %collective-permute-start.5 = (bf16[3,3,1,512,256]{4,3,2,1,0:T(8,128)(2,1)}, bf16[3,3,1,512,256]{4,3,2,1,0:T(8,128)(2,1)}, u32[]{:S(2)}, u32[]{:S(2)}) collective-permute-start(bf16[3,3,1,512,256]{4,3,2,1,0:T(8,128)(2,1)} %pad_maximum_fusion.2), channel_id=1, source_target_pairs={{1,0},{2,1},{3,2},{4,3},{5,4},{6,5},{7,6},{9,8},{10,9},{11,10},{12... | collective-permute-start | bytes 7077896 | tf_op jit(solution)/shard_map/ppermute | solution.py:283
  83.2 16.0 %collective-permute-done.4 = bf16[3,3,1,512,256]{4,3,2,1,0:T(8,128)(2,1)} collective-permute-done((bf16[3,3,1,512,256]{4,3,2,1,0:T(8,128)(2,1)}, bf16[3,3,1,512,256]{4,3,2,1,0:T(8,128)(2,1)}, u32[]{:S(2)}, u32[]{:S(2)}) %collective-permute-start.4) | collective-permute-done | bytes 2359328 | tf_op jit(solution)/shard_map/ppermute | solution.py:282
  101.0 6.0 %pad_maximum_fusion = bf16[3,3,3,512,256]{4,3,2,1,0:T(8,128)(2,1)} fusion(bf16[3,3,1,512,256]{4,3,2,1,0:T(8,128)(2,1)} %collective-permute-done.5, bf16[3,1,1,512,256]{4,3,2,1,0:T(8,128)(2,1)} %collective-permute-done.3, bf16[1,1,1,512,256]{4,3,2,1,0:T(8,128)(2,1)S(1)} %copy-done.8, bf16[1,1,1,512,256]{4,3,2,1,0:T(8,128)(2,1)S(1)} %bitcast.43, ...), kind=kLoop, calls=%fused_computation | loop fusion | flops 21233664 | bytes 14155776 | tf_op jit(solution)/shard_map/concatenate | solution.py:284
  106.9 84.4 %message_step.2 = (bf16[2304,256]{1,0:T(8,128)(2,1)}, bf16[2304,256]{1,0:T(8,128)(2,1)}, bf16[512,256]{1,0:T(8,128)(2,1)}) custom-call(s32[1]{0:T(128)} %constant.7.clone.1.refs_0_, s32[55296]{0:T(1024)} %reshape.57.refs_1_, bf16[27,512,256]{2,1,0:T(8,128)(2,1)} %bitcast.36, bf16[2304,256]{1,0:T(8,128)(2,1)} %get-tuple-element.12.refs_3_, ...), custom_call_target="tpu_custom_call" | custom-call | tf_op jit(solution)/shard_map/message_step/pallas_call | solution.py:252
  193.4 3.8 %collective-permute-start.7 = (bf16[1,1,1,512,256]{4,3,2,1,0:T(8,128)(2,1)}, bf16[1,1,1,512,256]{4,3,2,1,0:T(8,128)(2,1)S(1)}, u32[]{:S(2)}, u32[]{:S(2)}) collective-permute-start(bf16[1,1,1,512,256]{4,3,2,1,0:T(8,128)(2,1)} %bitcast.45), channel_id=1, source_target_pairs={{32,0},{64,32},{96,64},{33,1},{65,33},{97,65},{34,2},{66,34},{98,6... | collective-permute-start | bytes 786440 | tf_op jit(solution)/shard_map/ppermute | solution.py:283
  197.2 4.7 %collective-permute-done.6 = bf16[1,1,1,512,256]{4,3,2,1,0:T(8,128)(2,1)S(1)} collective-permute-done((bf16[1,1,1,512,256]{4,3,2,1,0:T(8,128)(2,1)}, bf16[1,1,1,512,256]{4,3,2,1,0:T(8,128)(2,1)S(1)}, u32[]{:S(2)}, u32[]{:S(2)}) %collective-permute-start.6) | collective-permute-done | bytes 262176 | tf_op jit(solution)/shard_map/ppermute | solution.py:282
  205.1 3.7 %collective-permute-start.8 = (bf16[3,1,1,512,256]{4,3,2,1,0:T(8,128)(2,1)S(1)}, bf16[3,1,1,512,256]{4,3,2,1,0:T(8,128)(2,1)S(1)}, u32[]{:S(2)}, u32[]{:S(2)}) collective-permute-start(bf16[3,1,1,512,256]{4,3,2,1,0:T(8,128)(2,1)S(1)} %pad_maximum_fusion.6), channel_id=1, source_target_pairs={{0,8},{8,16},{16,24},{1,9},{9,17},{17,25},{2,10},{10,18},{18,26},{... | collective-permute-start | bytes 2359304 | tf_op jit(solution)/shard_map/ppermute | solution.py:282
  210.1 15.7 %collective-permute-done.8 = bf16[3,1,1,512,256]{4,3,2,1,0:T(8,128)(2,1)S(1)} collective-permute-done((bf16[3,1,1,512,256]{4,3,2,1,0:T(8,128)(2,1)S(1)}, bf16[3,1,1,512,256]{4,3,2,1,0:T(8,128)(2,1)S(1)}, u32[]{:S(2)}, u32[]{:S(2)}) %collective-permute-start.8) | collective-permute-done | bytes 786464 | tf_op jit(solution)/shard_map/ppermute | solution.py:282
  225.8 4.2 %collective-permute-done.9 = bf16[3,1,1,512,256]{4,3,2,1,0:T(8,128)(2,1)S(1)} collective-permute-done((bf16[3,1,1,512,256]{4,3,2,1,0:T(8,128)(2,1)S(1)}, bf16[3,1,1,512,256]{4,3,2,1,0:T(8,128)(2,1)S(1)}, u32[]{:S(2)}, u32[]{:S(2)}) %collective-permute-start.9) | collective-permute-done | bytes 786464 | tf_op jit(solution)/shard_map/ppermute | solution.py:283
  233.1 3.6 %collective-permute-start.11 = (bf16[3,3,1,512,256]{4,3,2,1,0:T(8,128)(2,1)S(1)}, bf16[3,3,1,512,256]{4,3,2,1,0:T(8,128)(2,1)S(1)}, u32[]{:S(2)}, u32[]{:S(2)}) collective-permute-start(bf16[3,3,1,512,256]{4,3,2,1,0:T(8,128)(2,1)S(1)} %pad_maximum_fusion.3), channel_id=1, source_target_pairs={{1,0},{2,1},{3,2},{4,3},{5,4},{6,5},{7,6},{9,8},{10,9},{11,10},{12... | collective-permute-start | bytes 7077896 | tf_op jit(solution)/shard_map/ppermute | solution.py:283
  236.7 24.6 %collective-permute-done.10 = bf16[3,3,1,512,256]{4,3,2,1,0:T(8,128)(2,1)S(1)} collective-permute-done((bf16[3,3,1,512,256]{4,3,2,1,0:T(8,128)(2,1)S(1)}, bf16[3,3,1,512,256]{4,3,2,1,0:T(8,128)(2,1)S(1)}, u32[]{:S(2)}, u32[]{:S(2)}) %collective-permute-start.10) | collective-permute-done | bytes 2359328 | tf_op jit(solution)/shard_map/ppermute | solution.py:282
  263.1 3.3 pad_maximum_fusion.1
  266.4 81.9 %message_step.3 = bf16[2304,256]{1,0:T(8,128)(2,1)} custom-call(s32[1]{0:T(128)} %constant.7.clone.1.refs_0_, s32[55296]{0:T(1024)} %reshape.57.refs_1_, bf16[27,512,256]{2,1,0:T(8,128)(2,1)} %bitcast.35, bf16[2304,256]{1,0:T(8,128)(2,1)} %get-tuple-element.15.refs_3_, bf16[2304,256]{1,0:T(8,128)(2,1)} %get-tuple-element.16.refs_4_, ...), custom_call_target="tpu_custom_call" | custom-call | tf_op jit(solution)/shard_map/message_step/pallas_call | solution.py:252
  (78 shorter events, 34.4 us)
Async XLA Ops:
  4.2 18.1 %all-to-all-start = ((bf16[128,2,384]{2,1,0:T(2,128)(2,1)}), bf16[128,2,384]{2,1,0:T(2,128)(2,1)S(1)}, u32[]{:S(2)}, u32[]{:S(2)}) async-start(bf16[128,2,384]{2,1,0:T(2,128)(2,1)} %reshape.58), calls=%async_computation | async-start | bytes 393216 | tf_op jit(solution)/shard_map/all_to_all | solution.py:336
  14.5 32.5 %copy-start.15 = (f32[2,256]{1,0:T(2,128)S(1)}, f32[2,256]{1,0:T(2,128)}, u32[]{:S(2)}) copy-start(f32[2,256]{1,0:T(2,128)} %param.31) | copy-start | bytes 6148
  14.5 32.5 %copy-start.16 = (f32[2,256]{1,0:T(2,128)S(1)}, f32[2,256]{1,0:T(2,128)}, u32[]{:S(2)}) copy-start(f32[2,256]{1,0:T(2,128)} %param.30) | copy-start | bytes 6148
  14.5 33.1 %copy-start.13 = (s32[2304,24]{0,1:T(8,128)S(1)}, s32[2304,24]{0,1:T(8,128)}, u32[]{:S(2)}) copy-start(s32[2304,24]{0,1:T(8,128)} %param.21) | copy-start | bytes 663556
  22.4 24.7 %copy-start.10 = (bf16[256,384]{1,0:T(8,128)(2,1)}, bf16[256,384]{1,0:T(8,128)(2,1)S(1)}, u32[]{:S(2)}) copy-start(bf16[256,384]{1,0:T(8,128)(2,1)S(1)} %reshape.59) | copy-start | bytes 589828
  28.0 38.0 %copy-start.2 = (bf16[512,256]{1,0:T(8,128)(2,1)S(1)}, bf16[512,256]{1,0:T(8,128)(2,1)}, u32[]{:S(2)}) copy-start(bf16[512,256]{1,0:T(8,128)(2,1)} %get-tuple-element.11) | copy-start | bytes 786436
  28.0 10.6 %collective-permute-start = (bf16[1,1,1,512,256]{4,3,2,1,0:T(8,128)(2,1)}, bf16[1,1,1,512,256]{4,3,2,1,0:T(8,128)(2,1)S(1)}, u32[]{:S(2)}, u32[]{:S(2)}) collective-permute-start(bf16[1,1,1,512,256]{4,3,2,1,0:T(8,128)(2,1)} %bitcast.39), channel_id=1, source_target_pairs={{0,32},{32,64},{64,96},{1,33},{33,65},{65,97},{2,34},{34,66},{66,9... | collective-permute-start | bytes 786440 | tf_op jit(solution)/shard_map/ppermute | solution.py:282
  31.1 10.1 %collective-permute-start.1 = (bf16[1,1,1,512,256]{4,3,2,1,0:T(8,128)(2,1)}, bf16[1,1,1,512,256]{4,3,2,1,0:T(8,128)(2,1)S(1)}, u32[]{:S(2)}, u32[]{:S(2)}) collective-permute-start(bf16[1,1,1,512,256]{4,3,2,1,0:T(8,128)(2,1)} %bitcast.40), channel_id=1, source_target_pairs={{32,0},{64,32},{96,64},{33,1},{65,33},{97,65},{34,2},{66,34},{98,6... | collective-permute-start | bytes 786440 | tf_op jit(solution)/shard_map/ppermute | solution.py:283
  43.3 18.6 %collective-permute-start.2 = (bf16[3,1,1,512,256]{4,3,2,1,0:T(8,128)(2,1)}, bf16[3,1,1,512,256]{4,3,2,1,0:T(8,128)(2,1)S(1)}, u32[]{:S(2)}, u32[]{:S(2)}) collective-permute-start(bf16[3,1,1,512,256]{4,3,2,1,0:T(8,128)(2,1)} %pad_maximum_fusion.5), channel_id=1, source_target_pairs={{0,8},{8,16},{16,24},{1,9},{9,17},{17,25},{2,10},{10,18},{18,26},{... | collective-permute-start | bytes 2359304 | tf_op jit(solution)/shard_map/ppermute | solution.py:282
  45.7 20.3 %collective-permute-start.3 = (bf16[3,1,1,512,256]{4,3,2,1,0:T(8,128)(2,1)}, bf16[3,1,1,512,256]{4,3,2,1,0:T(8,128)(2,1)}, u32[]{:S(2)}, u32[]{:S(2)}) collective-permute-start(bf16[3,1,1,512,256]{4,3,2,1,0:T(8,128)(2,1)} %pad_maximum_fusion.5), channel_id=1, source_target_pairs={{8,0},{16,8},{24,16},{9,1},{17,9},{25,17},{10,2},{18,10},{26,18},{... | collective-permute-start | bytes 2359304 | tf_op jit(solution)/shard_map/ppermute | solution.py:283
  48.0 18.0 %copy-start.4 = (bf16[1,1,1,512,256]{4,3,2,1,0:T(8,128)(2,1)S(1)}, bf16[1,1,1,512,256]{4,3,2,1,0:T(8,128)(2,1)}, u32[]{:S(2)}) copy-start(bf16[1,1,1,512,256]{4,3,2,1,0:T(8,128)(2,1)} %copy-done.3) | copy-start | bytes 786436
  48.2 26.1 %copy-start.21 = (s32[128]{0:T(128)S(1)}, s32[128]{0:T(128)}, u32[]{:S(2)}) copy-start(s32[128]{0:T(128)} %param.18) | copy-start | bytes 1540
  68.6 30.6 %collective-permute-start.4 = (bf16[3,3,1,512,256]{4,3,2,1,0:T(8,128)(2,1)}, bf16[3,3,1,512,256]{4,3,2,1,0:T(8,128)(2,1)}, u32[]{:S(2)}, u32[]{:S(2)}) collective-permute-start(bf16[3,3,1,512,256]{4,3,2,1,0:T(8,128)(2,1)} %pad_maximum_fusion.2), channel_id=1, source_target_pairs={{0,1},{1,2},{2,3},{3,4},{4,5},{5,6},{6,7},{8,9},{9,10},{10,11},{11... | collective-permute-start | bytes 7077896 | tf_op jit(solution)/shard_map/ppermute | solution.py:282
  70.7 30.3 %collective-permute-start.5 = (bf16[3,3,1,512,256]{4,3,2,1,0:T(8,128)(2,1)}, bf16[3,3,1,512,256]{4,3,2,1,0:T(8,128)(2,1)}, u32[]{:S(2)}, u32[]{:S(2)}) collective-permute-start(bf16[3,3,1,512,256]{4,3,2,1,0:T(8,128)(2,1)} %pad_maximum_fusion.2), channel_id=1, source_target_pairs={{1,0},{2,1},{3,2},{4,3},{5,4},{6,5},{7,6},{9,8},{10,9},{11,10},{12... | collective-permute-start | bytes 7077896 | tf_op jit(solution)/shard_map/ppermute | solution.py:283
  80.1 20.9 %copy-start.1 = (bf16[3,1,1,512,256]{4,3,2,1,0:T(8,128)(2,1)S(1)}, bf16[3,1,1,512,256]{4,3,2,1,0:T(8,128)(2,1)}, u32[]{:S(2)}) copy-start(bf16[3,1,1,512,256]{4,3,2,1,0:T(8,128)(2,1)} %copy-done) | copy-start | bytes 2359300
  80.1 20.9 %copy-start.5 = (bf16[1,1,1,512,256]{4,3,2,1,0:T(8,128)(2,1)S(1)}, bf16[1,1,1,512,256]{4,3,2,1,0:T(8,128)(2,1)}, u32[]{:S(2)}) copy-start(bf16[1,1,1,512,256]{4,3,2,1,0:T(8,128)(2,1)} %copy-done.3) | copy-start | bytes 786436
  80.1 20.9 %copy-start.8 = (bf16[1,1,1,512,256]{4,3,2,1,0:T(8,128)(2,1)S(1)}, bf16[1,1,1,512,256]{4,3,2,1,0:T(8,128)(2,1)}, u32[]{:S(2)}) copy-start(bf16[1,1,1,512,256]{4,3,2,1,0:T(8,128)(2,1)} %copy-done.6) | copy-start | bytes 786436
  191.4 10.5 %collective-permute-start.6 = (bf16[1,1,1,512,256]{4,3,2,1,0:T(8,128)(2,1)}, bf16[1,1,1,512,256]{4,3,2,1,0:T(8,128)(2,1)S(1)}, u32[]{:S(2)}, u32[]{:S(2)}) collective-permute-start(bf16[1,1,1,512,256]{4,3,2,1,0:T(8,128)(2,1)} %bitcast.44), channel_id=1, source_target_pairs={{0,32},{32,64},{64,96},{1,33},{33,65},{65,97},{2,34},{34,66},{66,9... | collective-permute-start | bytes 786440 | tf_op jit(solution)/shard_map/ppermute | solution.py:282
  193.4 10.6 %collective-permute-start.7 = (bf16[1,1,1,512,256]{4,3,2,1,0:T(8,128)(2,1)}, bf16[1,1,1,512,256]{4,3,2,1,0:T(8,128)(2,1)S(1)}, u32[]{:S(2)}, u32[]{:S(2)}) collective-permute-start(bf16[1,1,1,512,256]{4,3,2,1,0:T(8,128)(2,1)} %bitcast.45), channel_id=1, source_target_pairs={{32,0},{64,32},{96,64},{33,1},{65,33},{97,65},{34,2},{66,34},{98,6... | collective-permute-start | bytes 786440 | tf_op jit(solution)/shard_map/ppermute | solution.py:283
  205.1 58.0 %copy-start.9 = (bf16[512,256]{1,0:T(8,128)(2,1)S(1)}, bf16[512,256]{1,0:T(8,128)(2,1)}, u32[]{:S(2)}) copy-start(bf16[512,256]{1,0:T(8,128)(2,1)} %get-tuple-element.14) | copy-start | bytes 786436
  205.1 20.7 %collective-permute-start.8 = (bf16[3,1,1,512,256]{4,3,2,1,0:T(8,128)(2,1)S(1)}, bf16[3,1,1,512,256]{4,3,2,1,0:T(8,128)(2,1)S(1)}, u32[]{:S(2)}, u32[]{:S(2)}) collective-permute-start(bf16[3,1,1,512,256]{4,3,2,1,0:T(8,128)(2,1)S(1)} %pad_maximum_fusion.6), channel_id=1, source_target_pairs={{0,8},{8,16},{16,24},{1,9},{9,17},{17,25},{2,10},{10,18},{18,26},{... | collective-permute-start | bytes 2359304 | tf_op jit(solution)/shard_map/ppermute | solution.py:282
  208.8 21.2 %collective-permute-start.9 = (bf16[3,1,1,512,256]{4,3,2,1,0:T(8,128)(2,1)S(1)}, bf16[3,1,1,512,256]{4,3,2,1,0:T(8,128)(2,1)S(1)}, u32[]{:S(2)}, u32[]{:S(2)}) collective-permute-start(bf16[3,1,1,512,256]{4,3,2,1,0:T(8,128)(2,1)S(1)} %pad_maximum_fusion.6), channel_id=1, source_target_pairs={{8,0},{16,8},{24,16},{9,1},{17,9},{25,17},{10,2},{18,10},{26,18},{... | collective-permute-start | bytes 2359304 | tf_op jit(solution)/shard_map/ppermute | solution.py:283
  231.2 30.2 %collective-permute-start.10 = (bf16[3,3,1,512,256]{4,3,2,1,0:T(8,128)(2,1)S(1)}, bf16[3,3,1,512,256]{4,3,2,1,0:T(8,128)(2,1)S(1)}, u32[]{:S(2)}, u32[]{:S(2)}) collective-permute-start(bf16[3,3,1,512,256]{4,3,2,1,0:T(8,128)(2,1)S(1)} %pad_maximum_fusion.3), channel_id=1, source_target_pairs={{0,1},{1,2},{2,3},{3,4},{4,5},{5,6},{6,7},{8,9},{9,10},{10,11},{11... | collective-permute-start | bytes 7077896 | tf_op jit(solution)/shard_map/ppermute | solution.py:282
  233.1 30.0 %collective-permute-start.11 = (bf16[3,3,1,512,256]{4,3,2,1,0:T(8,128)(2,1)S(1)}, bf16[3,3,1,512,256]{4,3,2,1,0:T(8,128)(2,1)S(1)}, u32[]{:S(2)}, u32[]{:S(2)}) collective-permute-start(bf16[3,3,1,512,256]{4,3,2,1,0:T(8,128)(2,1)S(1)} %pad_maximum_fusion.3), channel_id=1, source_target_pairs={{1,0},{2,1},{3,2},{4,3},{5,4},{6,5},{7,6},{9,8},{10,9},{11,10},{12... | collective-permute-start | bytes 7077896 | tf_op jit(solution)/shard_map/ppermute | solution.py:283
  (11 other events, 123.0 us)

commit v2 on v1

--- a/solution.py
+++ b/solution.py
@@ -124,10 +124,14 @@
     gathered = (even, odd)
     ghost_blocks, ghost_rows = ghosts.shape[0], ghosts.shape[1]
 
-    def fetch(block, slot):
-        return pltpu.make_async_copy(ghosts.at[block], staged.at[slot], sems.at[slot])
-
-    fetch(0, 0).start()
+    centre = ghost_blocks // 2
+
+    def fetch(block):
+        return pltpu.make_async_copy(ghosts.at[block], staged.at[block], sems.at[block])
+
+    for block in range(ghost_blocks):
+        if block != centre:
+            fetch(block).start()
 
     @pl.loop(0, rows // NODE_ROWS)
     def _(i):
@@ -144,16 +148,12 @@
 
     @pl.loop(0, ghost_blocks)
     def _(block):
-        slot = lax.rem(block, 2)
-        fetch(block, slot).wait()
-
-        @pl.when(block + 1 < ghost_blocks)
+        @pl.when(block != centre)
         def _():
-            fetch(block + 1, 1 - slot).start()
-
-        for piece in range(ghost_rows // NODE_ROWS):
-            values = staged[slot, pl.ds(piece * NODE_ROWS, NODE_ROWS), :].astype(F32)
-            store_split(pairs, pl.multiple_of(rows + block * ghost_rows + piece * NODE_ROWS, NODE_ROWS), values)
+            fetch(block).wait()
+            for piece in range(ghost_rows // NODE_ROWS):
+                values = staged[block, pl.ds(piece * NODE_ROWS, NODE_ROWS), :].astype(F32)
+                store_split(pairs, pl.multiple_of(rows + block * ghost_rows + piece * NODE_ROWS, NODE_ROWS), values)
 
     def gather(into, block, start, stop):
         base = pl.multiple_of(block * edges, HALF)
@@ -263,32 +263,118 @@
             pltpu.VMEM((edges, width), F32),
             pltpu.VMEM((edges, HALF), F32),
             pltpu.VMEM((width, width), BF16),
-            pltpu.VMEM((2, ghosts.shape[1], width), BF16),
+            pltpu.VMEM(ghosts.shape, BF16),
             pltpu.VMEM((2 * 64, HALF), F32),
-            pltpu.SemaphoreType.DMA((2,)),
+            pltpu.SemaphoreType.DMA((ghosts.shape[0],)),
         ],
         compiler_params=pltpu.CompilerParams(vmem_limit_bytes=VMEM_BYTES),
         name="message_step",
     )(block_total, edge_ids, ghosts, table, projected, floor, living, *weights, *extra)
 
 
-def with_halo(x, sides, width):
-    for axis, dim in sides:
-        devices, length = (lax.axis_size(axis), x.shape[dim])
-        up = [(i, i + 1) for i in range(devices - 1)]
-        down = [(j, i) for i, j in up]
-        last = lax.slice_in_dim(x, length - width, length, axis=dim)
-        first = lax.slice_in_dim(x, 0, width, axis=dim)
-        before = lax.ppermute(last, axis, up)
-        after = lax.ppermute(first, axis, down)
-        x = jnp.concatenate([before, x, after], axis=dim)
-    return x
+def exchange_kernel(axes, boundary, ghosts, send_sems, recv_sems):
+    place = [lax.axis_index(a) for a in axes]
+    sizes = [lax.axis_size(a) for a in axes]
+
+    def inside(axis, step):
+        return jnp.logical_and(place[axis] + step >= 0, place[axis] + step < sizes[axis])
+
+    def target(axis, step):
+        return tuple(place[a] + (step if a == axis else 0) for a in range(3))
+
+    barrier = pltpu.get_barrier_semaphore()
+    friends = jnp.int32(0)
+    for axis in range(3):
+        for step in (-1, 1):
+            friends = friends + inside(axis, step).astype(jnp.int32)
+
+            @pl.when(inside(axis, step))
+            def _():
+                pl.semaphore_signal(
+                    barrier, inc=1, device_id=target(axis, step), device_id_type=pl.DeviceIdType.MESH
+                )
+
+    pl.semaphore_wait(barrier, friends)
+
+    def number(offset):
+        return 9 * (offset[0] + 1) + 3 * (offset[1] + 1) + offset[2] + 1
+
+    def moved(offset, axis, step):
+        return tuple(offset[a] + (step if a == axis else 0) for a in range(3))
+
+    def send(offset, axis, step):
+        slot = number(moved(offset, axis, -step))
+        source = boundary if offset == (0, 0, 0) else ghosts.at[number(offset)]
+        return pltpu.make_async_remote_copy(
+            src_ref=source,
+            dst_ref=ghosts.at[slot],
+            send_sem=send_sems.at[slot],
+            recv_sem=recv_sems.at[slot],
+            device_id=target(axis, step),
+            device_id_type=pl.DeviceIdType.MESH,
+        )
+
+    def present(offset):
+        found = None
+        for a in range(3):
+            if offset[a] != 0:
+                here = inside(a, offset[a])
+                found = here if found is None else jnp.logical_and(found, here)
+        return found
+
+    def forward(offset, first_axis):
+        for axis in range(first_axis, 3):
+            for step in (-1, 1):
+
+                @pl.when(inside(axis, step))
+                def _():
+                    send(offset, axis, step).start()
+
+    def arrive(offset):
+        axis = max(a for a in range(3) if offset[a] != 0)
+        send(moved(offset, axis, -offset[axis]), axis, -offset[axis]).wait_recv()
+
+    middle = [(dx, 0, 0) for dx in (-1, 1)]
+    sides = [(dx, dy, 0) for dx in (0, -1, 1) for dy in (-1, 1)]
+    ends = [(dx, dy, dz) for dx in (0, -1, 1) for dy in (0, -1, 1) for dz in (-1, 1)]
+    forward((0, 0, 0), 0)
+    for offset in middle + sides:
+
+        @pl.when(present(offset))
+        def _():
+            arrive(offset)
+            forward(offset, 1 if offset in middle else 2)
+
+    for offset in ends:
+
+        @pl.when(present(offset))
+        def _():
+            arrive(offset)
+
+    for offset, first_axis in [((0, 0, 0), 0)] + [(o, 1) for o in middle] + [(o, 2) for o in sides]:
+        for axis in range(first_axis, 3):
+            for step in (-1, 1):
+                there = inside(axis, step)
+                if offset != (0, 0, 0):
+                    there = jnp.logical_and(there, present(offset))
+
+                @pl.when(there)
+                def _():
+                    send(offset, axis, step).wait_send()
 
 
 def exchange(boundary):
-    count, width = boundary.shape
-    spread = with_halo(boundary.reshape(1, 1, 1, count, width), (("gx", 0), ("gy", 1), ("gz", 2)), 1)
-    return spread.reshape(-1, count, width)
+    axes = ("gx", "gy", "gz")
+    anywhere = pl.BlockSpec(memory_space=pl.ANY)
+    return pl.pallas_call(
+        functools.partial(exchange_kernel, axes),
+        out_shape=jax.ShapeDtypeStruct((27,) + boundary.shape, boundary.dtype),
+        in_specs=[anywhere],
+        out_specs=anywhere,
+        scratch_shapes=[pltpu.SemaphoreType.DMA((27,)), pltpu.SemaphoreType.DMA((27,))],
+        compiler_params=pltpu.CompilerParams(collective_id=0, has_side_effects=True),
+        name="exchange",
+    )(boundary)
 
 
 def pick_rows(source_rows, row_ids):

time: 355 us -> 221 us (0.62)
  the two profiles are of different devices: /device:TPU:18 before, /device:TPU:49 now
where the time goes in v2:
time: 221 us
  Pallas kernels  196 us (89%)
  starting transfers between devices  10.4 us (5%)
  local copies, waits for them, and re-layouts  6.85 us (3%)
  other arithmetic  5.35 us (2%)
    pallas_call x2, Pallas kernels, message_step(): pl.pallas_call(functools.partial(step_kernel, slots, last), out_shape=tup...  122 us
    pallas_call x2, Pallas kernels, exchange(): pl.pallas_call(functools.partial(exchange_kernel, axes), out_shape=jax.Sh...  68.9 us
    all_to_all x1, starting transfers between devices, local(): lax.all_to_all(outgoing.reshape(devices, capacity, width + HALF), axes, s...  10.4 us
    pallas_call x1, Pallas kernels, open_table(): pl.pallas_call(open_kernel, out_shape=(jax.ShapeDtypeStruct((rows, width)...  4.93 us
  transfers between devices with their start and end apart: 1, of which 0 were waited for; matrix products, arithmetic and copies ran while one was open for 4% of the time, Pallas kernels for 0%

profile of v2, /device:TPU:49, one launch (start us, length us, event | category | flops | bytes accessed | tf_op | source)
XLA Modules:
  0.0 220.8 jit_solution(8786898848608134399)
XLA Ops:
  0.0 0.9 convert_reduce_fusion
  0.9 0.7 multiply_add_fusion
  1.6 1.6 convolution_convert_fusion.1
  3.4 0.8 reshape.46
  4.1 10.4 %all-to-all-start = ((bf16[128,2,384]{2,1,0:T(2,128)(2,1)}), bf16[128,2,384]{2,1,0:T(2,128)(2,1)S(1)}, u32[]{:S(2)}, u32[]{:S(2)}) async-start(bf16[128,2,384]{2,1,0:T(2,128)(2,1)} %reshape.46), calls=%async_computation | async-start | bytes 393216 | tf_op jit(solution)/shard_map/all_to_all | solution.py:422
  14.6 0.4 fusion.2
  15.0 0.4 copy.33
  15.3 1.2 compare_select_fusion.refs_5_
  17.4 0.4 copy.34
  17.8 0.9 reshape.45.refs_1_
  18.7 0.6 fusion.12
  19.3 0.6 fusion.10
  19.9 0.6 fusion.8
  20.5 0.8 slice_bitcast_fusion
  21.3 0.3 fusion.1
  21.7 1.0 slice_bitcast_fusion.1
  22.7 0.6 broadcast_multiply_fusion.halo_ids.refs_18_
  23.4 0.7 slice.104.arrived_ref
  24.1 4.9 %open_table.1 = (bf16[2304,256]{1,0:T(8,128)(2,1)}, bf16[2304,256]{1,0:T(8,128)(2,1)}, bf16[512,256]{1,0:T(8,128)(2,1)}) custom-call(bf16[2048,256]{1,0:T(8,128)(2,1)} %latent_ref.1, bf16[256,256]{1,0:T(8,128)(2,1)} %slice.104.arrived_ref, s32[512]{0:T(512)} %broadcast_multiply_fusion.halo_ids.refs_18_, bf16[256,256]{1,0:T(8,128)(2,1)} %get-tuple-element.44.weight_ref), custom_call_target="tpu_custom_call" | custom-call | tf_op jit(solution)/shard_map/open_table/pallas_call | solution.py:77
  29.0 35.0 %exchange.2.refs_2_ = bf16[27,512,256]{2,1,0:T(8,128)(2,1)} custom-call(bf16[512,256]{1,0:T(8,128)(2,1)} %get-tuple-element.11.boundary), custom_call_target="tpu_custom_call" | custom-call | tf_op jit(solution)/shard_map/exchange/pallas_call | solution.py:369
  64.0 1.2 pad_maximum_fusion.refs_6_
  65.2 62.0 %message_step.2 = (bf16[2304,256]{1,0:T(8,128)(2,1)}, bf16[2304,256]{1,0:T(8,128)(2,1)}, bf16[512,256]{1,0:T(8,128)(2,1)}) custom-call(s32[1]{0:T(128)} %constant.7.clone.1.refs_0_, s32[55296]{0:T(1024)} %reshape.45.refs_1_, bf16[27,512,256]{2,1,0:T(8,128)(2,1)} %exchange.2.refs_2_, bf16[2304,256]{1,0:T(8,128)(2,1)} %get-tuple-element.12.refs_3_, ...), custom_call_target="tpu_custom_call" | custom-call | tf_op jit(solution)/shard_map/message_step/pallas_call | solution.py:252
  127.2 33.9 %exchange.3.refs_2_ = bf16[27,512,256]{2,1,0:T(8,128)(2,1)} custom-call(bf16[512,256]{1,0:T(8,128)(2,1)} %get-tuple-element.14.boundary), custom_call_target="tpu_custom_call" | custom-call | tf_op jit(solution)/shard_map/exchange/pallas_call | solution.py:369
  161.2 59.6 %message_step.3 = bf16[2304,256]{1,0:T(8,128)(2,1)} custom-call(s32[1]{0:T(128)} %constant.7.clone.1.refs_0_, s32[55296]{0:T(1024)} %reshape.45.refs_1_, bf16[27,512,256]{2,1,0:T(8,128)(2,1)} %exchange.3.refs_2_, bf16[2304,256]{1,0:T(8,128)(2,1)} %get-tuple-element.15.refs_3_, bf16[2304,256]{1,0:T(8,128)(2,1)} %get-tuple-element.16.refs_4_, ...), custom_call_target="tpu_custom_call" | custom-call | tf_op jit(solution)/shard_map/message_step/pallas_call | solution.py:252
  (32 shorter events, 0.5 us)
Async XLA Ops:
  0.0 14.6 %copy-start.12 = (s32[128]{0:T(128)S(1)}, s32[128]{0:T(128)}, u32[]{:S(2)}) copy-start(s32[128]{0:T(128)} %param.18) | copy-start | bytes 1540
  0.0 14.9 %copy-start.4 = (s32[2304,24]{0,1:T(8,128)S(1)}, s32[2304,24]{0,1:T(8,128)}, u32[]{:S(2)}) copy-start(s32[2304,24]{0,1:T(8,128)} %param.21) | copy-start | bytes 663556
  4.1 19.2 %all-to-all-start = ((bf16[128,2,384]{2,1,0:T(2,128)(2,1)}), bf16[128,2,384]{2,1,0:T(2,128)(2,1)S(1)}, u32[]{:S(2)}, u32[]{:S(2)}) async-start(bf16[128,2,384]{2,1,0:T(2,128)(2,1)} %reshape.46), calls=%async_computation | async-start | bytes 393216 | tf_op jit(solution)/shard_map/all_to_all | solution.py:422
  17.3 1.4 copy-start.6
  17.3 1.4 copy-start.7
  17.3 2.0 copy-start.8
  17.3 2.0 copy-start.9
  17.3 2.5 %copy-start.10 = (f32[2,256]{1,0:T(2,128)S(1)}, f32[2,256]{1,0:T(2,128)}, u32[]{:S(2)}) copy-start(f32[2,256]{1,0:T(2,128)} %param.31) | copy-start | bytes 6148
  17.4 2.5 %copy-start.11 = (f32[2,256]{1,0:T(2,128)S(1)}, f32[2,256]{1,0:T(2,128)}, u32[]{:S(2)}) copy-start(f32[2,256]{1,0:T(2,128)} %param.30) | copy-start | bytes 6148
  17.4 3.1 %copy-start.2 = (bf16[2,256,256]{2,1,0:T(8,128)(2,1)S(1)}, bf16[2,256,256]{2,1,0:T(8,128)(2,1)}, u32[]{:S(2)}) copy-start(bf16[2,256,256]{2,1,0:T(8,128)(2,1)} %param.29) | copy-start | bytes 786436
  17.4 3.1 %copy-start.3 = (bf16[2,256,256]{2,1,0:T(8,128)(2,1)S(1)}, bf16[2,256,256]{2,1,0:T(8,128)(2,1)}, u32[]{:S(2)}) copy-start(bf16[2,256,256]{2,1,0:T(8,128)(2,1)} %param.24) | copy-start | bytes 786436
  18.7 3.0 %copy-start = (bf16[2,2,256,256]{3,2,1,0:T(8,128)(2,1)S(1)}, bf16[2,2,256,256]{3,2,1,0:T(8,128)(2,1)}, u32[]{:S(2)}) copy-start(bf16[2,2,256,256]{3,2,1,0:T(8,128)(2,1)} %param.27) | copy-start | bytes 1572868
  18.7 3.0 %copy-start.1 = (bf16[2,2,256,256]{3,2,1,0:T(8,128)(2,1)S(1)}, bf16[2,2,256,256]{3,2,1,0:T(8,128)(2,1)}, u32[]{:S(2)}) copy-start(bf16[2,2,256,256]{3,2,1,0:T(8,128)(2,1)} %param.22) | copy-start | bytes 1572868
  21.7 1.0 copy-start.5

commit v3 on v1

v3 whole, which is shorter than its diff:
```python
import functools

import jax
import jax.numpy as jnp
from jax import lax
from jax.experimental import pallas as pl
from jax.experimental.pallas import tpu as pltpu
from jax.sharding import PartitionSpec as P

EPS = 1e-05
F32 = jnp.float32
BF16 = jnp.bfloat16
HALF = 128
ROWS = 32
CHUNK = 256
GROUP = 8
NODE_ROWS = 256
AXES = ("gx", "gy", "gz")
MESH = pl.DeviceIdType.MESH
VMEM_BYTES = 58 * 2**20
VMEM = pl.BlockSpec(memory_space=pltpu.VMEM)
SMEM = pl.BlockSpec(memory_space=pltpu.SMEM)
ANYWHERE = pl.BlockSpec(memory_space=pl.ANY)


def layer_norm(values, feature_gain):
    average = jnp.mean(values, axis=-1, keepdims=True)
    centred = values - average
    spread = jnp.mean(centred * centred, axis=-1, keepdims=True)
    return centred * lax.rsqrt(spread + EPS) * feature_gain


def store_split(pairs, first_row, values):
    count = values.shape[0]
    pairs[pl.ds(2 * first_row, count, stride=2), :] = values[:, :HALF]
    pairs[pl.ds(2 * first_row + 1, count, stride=2), :] = values[:, HALF:]


def load_split(pairs, first_row, count):
    left = pairs[pl.ds(2 * first_row, count, stride=2), :]
    right = pairs[pl.ds(2 * first_row + 1, count, stride=2), :]
    return jnp.concatenate([left, right], axis=1)


def project(rows, weight):
    return jnp.dot(rows, weight, preferred_element_type=F32).astype(BF16)


def copy_rows(source, ids, into, count):
    @pl.loop(0, count // 64)
    def _(block):
        for g in range(64 // GROUP):
            some = ids.at[pl.ds(block * 64 + g * GROUP, GROUP)]
            for e in range(GROUP):
                row = pl.multiple_of(some[e], 2)
                place = pl.multiple_of(2 * (block * 64 + g * GROUP + e), 2)
                into[pl.ds(place, 2), :] = source[pl.ds(row, 2), :]


def order_kernel(neighbours, digits, halo_lanes, edge_ids, floor_ref, order_ref, place_ref, count_ref, places):
    rows, slots = neighbours.shape
    boundary = halo_lanes.shape[1]
    n = NODE_ROWS
    lower = (
        lax.broadcasted_iota(jnp.int32, (n, n), 0) > lax.broadcasted_iota(jnp.int32, (n, n), 1)
    ).astype(BF16)
    lane = lax.broadcasted_iota(jnp.int32, (n, boundary), 1).astype(F32)

    def one_chunk(c, carry):
        used, spare = carry
        first = pl.multiple_of(c * n, n)
        active = jnp.max(neighbours[pl.ds(first, n), :], axis=1, keepdims=True) >= 0
        row_ids = lax.broadcasted_iota(jnp.int32, (n, boundary), 0) + first
        same = (row_ids == halo_lanes[...]).astype(F32)
        listed = jnp.sum(same, axis=1, keepdims=True) > 0.0
        position = jnp.sum(same * lane, axis=1, keepdims=True)
        others = jnp.where(listed, 0.0, jnp.where(active, 1.0, 0.0))
        idle = jnp.where(listed, 0.0, jnp.where(active, 0.0, 1.0))
        others = jnp.broadcast_to(others, (n, HALF))
        idle = jnp.broadcast_to(idle, (n, HALF))
        before = jnp.dot(lower, others.astype(BF16), preferred_element_type=F32) + used
        behind = jnp.dot(lower, idle.astype(BF16), preferred_element_type=F32) + spare
        place = jnp.where(others > 0.0, boundary + before, rows - 1 - behind)
        place = jnp.where(listed, position, place)
        places[pl.ds(first, n), :] = place
        place_ref[pl.ds(first, n), :] = (2.0 * place[:, :1]).astype(jnp.int32)
        return used + jnp.sum(others[:, :1]), spare + jnp.sum(idle[:, :1])

    used, _ = lax.fori_loop(0, rows // n, one_chunk, (jnp.float32(0.0), jnp.float32(0.0)))
    count_ref[0] = used.astype(jnp.int32) + boundary

    @pl.loop(0, rows // n)
    def _(c):
        first = pl.multiple_of(c * n, n)
        halves = []
        for half in range(n // HALF):
            lanes = lax.broadcasted_iota(jnp.int32, (rows, HALF), 1).astype(F32)
            wanted = lanes + (first + half * HALF).astype(F32)
            halves.append(jnp.where(places[...] == wanted, 1.0, 0.0).astype(BF16))
        chosen = jnp.concatenate(halves, axis=1)
        picked = jnp.dot(digits[...], chosen, preferred_element_type=F32)
        half_rows = digits.shape[0] // 2
        value = picked[:half_rows] * 128.0 + picked[half_rows:]
        here = pl.ds(first, n)
        edge_ids[:, here] = (2.0 * jnp.maximum(value[:slots] - 1.0, 0.0)).astype(jnp.int32)
        order_ref[:, here] = (2.0 * value[slots : slots + 1]).astype(jnp.int32)
        floor = jnp.where(value > 0.5, EPS, jnp.inf).astype(F32)
        floor_ref[here, :] = jnp.transpose(jnp.concatenate([floor] * (HALF // half_rows), axis=0))


def order_rows(neighbours, halo_rows):
    rows, slots = neighbours.shape
    half_rows = 32
    ids = neighbours.T + 1
    ids = jnp.concatenate(
        [ids, jnp.arange(rows, dtype=jnp.int32)[None], jnp.zeros((half_rows - slots - 1, rows), jnp.int32)]
    )
    digits = jnp.concatenate([ids // 128, ids % 128]).astype(BF16)
    return pl.pallas_call(
        order_kernel,
        out_shape=(
            jax.ShapeDtypeStruct((slots, rows), jnp.int32),
            jax.ShapeDtypeStruct((rows, HALF), F32),
            jax.ShapeDtypeStruct((1, rows), jnp.int32),
            jax.ShapeDtypeStruct((rows, 1), jnp.int32),
            jax.ShapeDtypeStruct((1,), jnp.int32),
        ),
        in_specs=[VMEM, VMEM, VMEM],
        out_specs=(VMEM, VMEM, VMEM, VMEM, SMEM),
        scratch_shapes=[pltpu.VMEM((rows, HALF), F32)],
        compiler_params=pltpu.CompilerParams(vmem_limit_bytes=VMEM_BYTES),
        name="order_rows",
    )(neighbours, digits, halo_rows[None, :])


def open_kernel(latent_ref, arrived_ref, halo_ids, order, weight_ref, ordered_ref, projected_ref, boundary_ref, pairs, picked):
    local_rows = latent_ref.shape[0]
    arrivals = arrived_ref.shape[0]
    rows = local_rows + arrivals

    def sources(take):
        @pl.loop(0, local_rows // NODE_ROWS)
        def _(i):
            first = pl.multiple_of(i * NODE_ROWS, NODE_ROWS)
            take(first, latent_ref[pl.ds(first, NODE_ROWS), :])

        take(local_rows, arrived_ref[...])

    def projection(first, values):
        projected = project(values, weight_ref[...])
        projected_ref[pl.ds(first, NODE_ROWS), :] = projected
        store_split(pairs, first, projected.astype(F32))

    sources(projection)
    count = boundary_ref.shape[0]
    copy_rows(pairs, halo_ids, picked, count)
    boundary_ref[...] = load_split(picked, 0, count).astype(BF16)
    sources(lambda first, values: store_split(pairs, first, values.astype(F32)))
    copy_rows(pairs, order, picked, rows)

    @pl.loop(0, rows // NODE_ROWS)
    def _(i):
        first = pl.multiple_of(i * NODE_ROWS, NODE_ROWS)
        ordered_ref[pl.ds(first, NODE_ROWS), :] = load_split(picked, first, NODE_ROWS).astype(BF16)


def open_table(latent, arrived, halo_ids, order, weight):
    rows = latent.shape[0] + arrived.shape[0]
    width = latent.shape[1]
    count = halo_ids.shape[0]
    return pl.pallas_call(
        open_kernel,
        out_shape=(
            jax.ShapeDtypeStruct((rows, width), BF16),
            jax.ShapeDtypeStruct((rows, width), BF16),
            jax.ShapeDtypeStruct((count, width), BF16),
        ),
        in_specs=[VMEM, VMEM, SMEM, SMEM, VMEM],
        out_specs=(VMEM, VMEM, VMEM),
        scratch_shapes=[pltpu.VMEM((2 * rows, HALF), F32), pltpu.VMEM((2 * rows, HALF), F32)],
        compiler_params=pltpu.CompilerParams(vmem_limit_bytes=VMEM_BYTES),
        name="open_table",
    )(latent, arrived, halo_ids, order, weight)


class Grid:
    def __init__(self):
        self.place = [lax.axis_index(a) for a in AXES]
        self.sizes = [lax.axis_size(a) for a in AXES]

    def inside(self, axis, step):
        return jnp.logical_and(self.place[axis] + step >= 0, self.place[axis] + step < self.sizes[axis])

    def target(self, axis, step):
        return tuple(self.place[a] + (step if a == axis else 0) for a in range(3))

    def present(self, offset):
        found = None
        for a in range(3):
            if offset[a] != 0:
                here = self.inside(a, offset[a])
                found = here if found is None else jnp.logical_and(found, here)
        return found

    def greet(self):
        barrier = pltpu.get_barrier_semaphore()
        friends = jnp.int32(0)
        for axis in range(3):
            for step in (-1, 1):
                friends = friends + self.inside(axis, step).astype(jnp.int32)

                @pl.when(self.inside(axis, step))
                def _():
                    pl.semaphore_signal(barrier, inc=1, device_id=self.target(axis, step), device_id_type=MESH)

        pl.semaphore_wait(barrier, friends)


def number(offset):
    return 9 * (offset[0] + 1) + 3 * (offset[1] + 1) + offset[2] + 1


def moved(offset, axis, step):
    return tuple(offset[a] + (step if a == axis else 0) for a in range(3))


CENTRE = (0, 0, 0)
MIDDLE = [(dx, 0, 0) for dx in (-1, 1)]
SIDES = [(dx, dy, 0) for dx in (0, -1, 1) for dy in (-1, 1)]
ENDS = [(dx, dy, dz) for dx in (0, -1, 1) for dy in (0, -1, 1) for dz in (-1, 1)]


class Exchange:
    def __init__(self, grid, boundary, ghosts, send_sems, recv_sems):
        self.grid, self.boundary, self.ghosts = grid, boundary, ghosts
        self.send_sems, self.recv_sems = send_sems, recv_sems

    def copy(self, offset, axis, step):
        slot = number(moved(offset, axis, -step))
        return pltpu.make_async_remote_copy(
            src_ref=self.boundary if offset == CENTRE else self.ghosts.at[number(offset)],
            dst_ref=self.ghosts.at[slot],
            send_sem=self.send_sems.at[slot],
            recv_sem=self.recv_sems.at[slot],
            device_id=self.grid.target(axis, step),
            device_id_type=MESH,
        )

    def first_axis(self, offset):
        return 0 if offset == CENTRE else 1 if offset in MIDDLE else 2

    def forward(self, offset):
        for axis in range(self.first_axis(offset), 3):
            for step in (-1, 1):

                @pl.when(self.grid.inside(axis, step))
                def _():
                    self.copy(offset, axis, step).start()

    def arrive(self, offset):
        axis = max(a for a in range(3) if offset[a] != 0)
        self.copy(moved(offset, axis, -offset[axis]), axis, -offset[axis]).wait_recv()

    def relay(self, offsets):
        for offset in offsets:

            @pl.when(self.grid.present(offset))
            def _():
                self.arrive(offset)
                self.forward(offset)

    def finish_sends(self):
        for offset in [CENTRE] + MIDDLE + SIDES:
            for axis in range(self.first_axis(offset), 3):
                for step in (-1, 1):
                    there = self.grid.inside(axis, step)
                    if offset != CENTRE:
                        there = jnp.logical_and(there, self.grid.present(offset))

                    @pl.when(there)
                    def _():
                        self.copy(offset, axis, step).wait_send()


class EdgeLayers:
    def __init__(self, rows, slots, refs, scratch):
        self.edge_ids, self.floor = refs["edge_ids"], refs["floor"]
        self.refs = refs
        self.rows, self.slots = rows, slots
        self.edges = slots * ROWS
        self.pairs, self.buffers, self.receive, self.summed, self.raw, self.square, self.weight = scratch
        self.width = self.receive.shape[1]

    def prepare(self, table_ref):
        refs = self.refs
        wide = refs["edge_out"][...].astype(F32)
        self.weight[...] = (wide - jnp.mean(wide, axis=1, keepdims=True)).astype(BF16)

        @pl.loop(0, self.rows // NODE_ROWS)
        def _(i):
            here = pl.ds(pl.multiple_of(i * NODE_ROWS, NODE_ROWS), NODE_ROWS)
            self.summed[here, :] = jnp.zeros((NODE_ROWS, self.width), F32)
            self.receive[here, :] = (
                jnp.dot(table_ref[here, :], refs["receive_weight"][...], preferred_element_type=F32)
                + refs["edge_bias"][...]
            )

    def gather(self, into, block, start, stop):
        first = pl.multiple_of(block * ROWS, ROWS)
        for e in range(start, stop):
            k, r = divmod(e, ROWS)
            if r % GROUP == 0:
                ids = self.edge_ids.at[k, pl.ds(first + r, GROUP)]
            into[pl.ds(2 * e, 2), :] = self.pairs[pl.ds(ids[r % GROUP], 2), :]

    def first_half(self, source, first, chunk, shift):
        per_chunk = CHUNK // ROWS
        own = self.receive[pl.ds(first, ROWS), :]
        left = source[pl.ds(2 * chunk * CHUNK, CHUNK, stride=2), :].reshape(per_chunk, ROWS, HALF)
        right = source[pl.ds(2 * chunk * CHUNK + 1, CHUNK, stride=2), :].reshape(per_chunk, ROWS, HALF)
        left = jnp.maximum(left + own[:, :HALF][None], 0.0).reshape(CHUNK, HALF).astype(BF16)
        right = jnp.maximum(right + own[:, HALF:][None], 0.0).reshape(CHUNK, HALF).astype(BF16)
        active = jnp.concatenate([left, right], axis=1)
        centred = jnp.dot(active, self.weight[...], preferred_element_type=F32) + shift
        total = jnp.sum(
            centred[:, :HALF] * centred[:, :HALF] + centred[:, HALF:] * centred[:, HALF:], axis=1, keepdims=True
        )
        here = pl.ds(chunk * CHUNK, CHUNK)
        self.raw[here, :] = centred
        self.square[here, :] = jnp.broadcast_to(total, (CHUNK, HALF))

    def second_half(self, floor, chunk, sums):
        left, right = sums
        per_chunk = CHUNK // ROWS
        for k in range(chunk * per_chunk, (chunk + 1) * per_chunk):
            here = pl.ds(k * ROWS, ROWS)
            scale = lax.rsqrt(self.square[here, :] * (1.0 / self.width) + floor[:, k : k + 1])
            left = left + self.raw[here, :HALF] * scale
            right = right + self.raw[here, HALF:] * scale
        return left, right

    def one_block(self, block, parity, last_block):
        chunks = self.edges // CHUNK
        first = pl.multiple_of(block * ROWS, ROWS)
        following = jnp.minimum(block + 1, last_block)
        edge_shift = self.refs["edge_shift"]
        shift = edge_shift[...] - jnp.mean(edge_shift[...], axis=1, keepdims=True)
        floor = self.floor[pl.ds(first, ROWS), :]
        sums = (jnp.zeros((ROWS, HALF), F32), jnp.zeros((ROWS, HALF), F32))
        for chunk in range(chunks + 1):
            if chunk < chunks:
                self.gather(self.buffers[1 - parity], following, chunk * CHUNK, (chunk + 1) * CHUNK)
                self.first_half(self.buffers[parity], first, chunk, shift)
            if chunk > 0:
                sums = self.second_half(floor, chunk - 1, sums)
        self.summed[pl.ds(first, ROWS), :HALF] = sums[0]
        self.summed[pl.ds(first, ROWS), HALF:] = sums[1]


def node_layers(refs, table_ref, summed, here):
    own = table_ref[here, :]
    message = (summed[here, :] * refs["edge_gain"][...]).astype(BF16)
    hidden = (
        jnp.dot(own, refs["node_self"][...], preferred_element_type=F32)
        + jnp.dot(message, refs["node_message"][...], preferred_element_type=F32)
        + refs["node_bias"][...]
    )
    hidden = jnp.maximum(hidden, 0.0).astype(BF16)
    node_raw = jnp.dot(hidden, refs["node_out"][...], preferred_element_type=F32) + refs["node_shift"][...]
    return own.astype(F32) + layer_norm(node_raw, refs["node_gain"][...])


NAMES = (
    "edge_ids",
    "floor",
    "receive_weight",
    "edge_bias",
    "edge_out",
    "edge_shift",
    "edge_gain",
    "node_self",
    "node_message",
    "node_bias",
    "node_out",
    "node_shift",
    "node_gain",
)


def edge_scratch(rows, slots, senders, width):
    edges = slots * ROWS
    return [
        pltpu.VMEM((2 * senders, HALF), F32),
        pltpu.VMEM((2 * edges, HALF), F32),
        pltpu.VMEM((2 * edges, HALF), F32),
        pltpu.VMEM((rows, width), F32),
        pltpu.VMEM((rows, width), F32),
        pltpu.VMEM((edges, width), F32),
        pltpu.VMEM((edges, HALF), F32),
        pltpu.VMEM((width, width), BF16),
    ]


def unpack_scratch(scratch):
    pairs, even, odd, receive, summed, raw, square, weight = scratch
    return pairs, (even, odd), receive, summed, raw, square, weight


def spread_block(pairs, first_row, block_ref):
    @pl.loop(0, block_ref.shape[0] // 128)
    def _(piece):
        start = pl.multiple_of(piece * 128, 128)
        store_split(pairs, first_row + start, block_ref[pl.ds(start, 128), :].astype(F32))


def first_step_kernel(slots, blocks, marks, *args):
    refs = dict(zip(NAMES, args))
    table_ref, projected_ref, boundary_ref, next_weight = args[13:17]
    renewed_ref, next_projected, next_ghosts = args[17:20]
    scratch = unpack_scratch(args[20:28])
    ghosts, next_boundary, send_a, recv_a, send_b, recv_b = args[28:]
    pairs, summed = scratch[0], scratch[3]
    rows = table_ref.shape[0]
    boundary_rows = boundary_ref.shape[0]
    grid = Grid()
    now = Exchange(grid, boundary_ref, ghosts, send_a, recv_a)
    later = Exchange(grid, next_boundary, next_ghosts, send_b, recv_b)
    layers = EdgeLayers(rows, slots, refs, scratch)
    grid.greet()
    now.forward(CENTRE)
    layers.prepare(table_ref)

    @pl.loop(0, rows // NODE_ROWS)
    def _(i):
        first = pl.multiple_of(i * NODE_ROWS, NODE_ROWS)
        store_split(pairs, first, projected_ref[pl.ds(first, NODE_ROWS), :].astype(F32))

    def spread(offset):
        spread_block(pairs, rows + number(offset) * boundary_rows, ghosts.at[number(offset)])

    def spread_all(offsets):
        for offset in offsets:

            @pl.when(grid.present(offset))
            def _():
                spread(offset)

    now.relay(MIDDLE)
    now.relay(SIDES[:2])
    spread_all(MIDDLE)
    spread_all(SIDES[:2])
    now.relay(SIDES[2:])
    spread_all(SIDES[2:])
    for offset in ENDS:

        @pl.when(grid.present(offset))
        def _():
            now.arrive(offset)
            spread(offset)

    layers.gather(layers.buffers[0], 0, 0, layers.edges)

    def renew(first):
        here = pl.ds(first, NODE_ROWS)
        renewed = node_layers(refs, table_ref, summed, here).astype(BF16)
        renewed_ref[here, :] = renewed
        projected = project(renewed, next_weight[...])
        next_projected[here, :] = projected
        return projected

    @pl.loop(0, blocks // 2)
    def _(pair):
        @pl.when(pair == marks[0])
        def _():
            for first in range(0, boundary_rows, NODE_ROWS):
                next_boundary[pl.ds(first, NODE_ROWS), :] = renew(first)
            later.forward(CENTRE)

        for mark, offsets in zip(marks[1:], (MIDDLE, SIDES[:2], SIDES[2:])):

            @pl.when(pair == mark)
            def _():
                later.relay(offsets)

        for parity in range(2):
            block = 2 * pair + parity

            @pl.when(block < blocks + grid.place[0])
            def _():
                layers.one_block(block, parity, blocks - 1)

    @pl.loop(boundary_rows // NODE_ROWS, rows // NODE_ROWS)
    def _(i):
        renew(pl.multiple_of(i * NODE_ROWS, NODE_ROWS))

    for offset in ENDS:

        @pl.when(grid.present(offset))
        def _():
            later.arrive(offset)

    now.finish_sends()
    later.finish_sends()


def first_step(blocks, layer_args, table, projected, boundary, next_weight):
    rows, width = table.shape
    slots = layer_args[0].shape[0]
    count = boundary.shape[0]
    first_pair = count // ROWS // 2
    rest = blocks // 2 - first_pair
    marks = (first_pair, first_pair + rest * 5 // 26, first_pair + rest * 7 // 26, first_pair + rest * 14 // 26)
    return pl.pallas_call(
        functools.partial(first_step_kernel, slots, blocks, marks),
        out_shape=(
            jax.ShapeDtypeStruct((rows, width), BF16),
            jax.ShapeDtypeStruct((rows, width), BF16),
            jax.ShapeDtypeStruct((27, count, width), BF16),
        ),
        in_specs=[SMEM] + [VMEM] * 16,
        out_specs=(VMEM, VMEM, ANYWHERE),
        scratch_shapes=edge_scratch(rows, slots, rows + 27 * count, width)
        + [pltpu.VMEM((27, count, width), BF16), pltpu.VMEM((count, width), BF16)]
        + [pltpu.SemaphoreType.DMA((27,))] * 4,
        compiler_params=pltpu.CompilerParams(
            collective_id=0, has_side_effects=True, vmem_limit_bytes=VMEM_BYTES
        ),
        name="first_step",
    )(*layer_args, table, projected, boundary, next_weight)


def last_step_kernel(slots, *args):
    refs = dict(zip(NAMES, args))
    table_ref, projected_ref, ghosts, living_ref, place_ids, count_ref = args[13:19]
    updated_ref = args[19]
    scratch = unpack_scratch(args[20:28])
    staged, ordered, sems = args[28:]
    pairs, summed = scratch[0], scratch[3]
    rows = table_ref.shape[0]
    ghost_blocks, ghost_rows = ghosts.shape[0], ghosts.shape[1]
    centre = ghost_blocks // 2
    layers = EdgeLayers(rows, slots, refs, scratch)

    def fetch(block):
        return pltpu.make_async_copy(ghosts.at[block], staged.at[block], sems.at[block])

    for block in range(ghost_blocks):
        if block != centre:
            fetch(block).start()
    layers.prepare(table_ref)

    @pl.loop(0, rows // NODE_ROWS)
    def _(i):
        first = pl.multiple_of(i * NODE_ROWS, NODE_ROWS)
        store_split(ordered, first, projected_ref[pl.ds(first, NODE_ROWS), :].astype(F32))

    copy_rows(ordered, place_ids, pairs, rows)

    @pl.loop(0, ghost_blocks)
    def _(block):
        @pl.when(block != centre)
        def _():
            fetch(block).wait()
            spread_block(pairs, pl.multiple_of(rows + block * ghost_rows, ghost_rows), staged.at[block])

    blocks = (count_ref[0] + ROWS - 1) // ROWS
    layers.gather(layers.buffers[0], 0, 0, layers.edges)

    @pl.loop(0, (blocks + 1) // 2)
    def _(pair):
        for parity in range(2):
            block = 2 * pair + parity

            @pl.when(block < blocks)
            def _():
                layers.one_block(block, parity, rows // ROWS - 1)

    @pl.loop(0, rows // NODE_ROWS)
    def _(i):
        first = pl.multiple_of(i * NODE_ROWS, NODE_ROWS)
        renewed = node_layers(refs, table_ref, summed, pl.ds(first, NODE_ROWS))
        store_split(ordered, first, renewed)

    copy_rows(ordered, place_ids, pairs, rows)

    @pl.loop(0, rows // NODE_ROWS)
    def _(i):
        first = pl.multiple_of(i * NODE_ROWS, NODE_ROWS)
        here = pl.ds(first, NODE_ROWS)
        updated_ref[here, :] = (load_split(pairs, first, NODE_ROWS) * living_ref[here, :]).astype(BF16)


def last_step(layer_args, table, projected, ghosts, living, place_ids, count):
    rows, width = table.shape
    slots = layer_args[0].shape[0]
    return pl.pallas_call(
        functools.partial(last_step_kernel, slots),
        out_shape=jax.ShapeDtypeStruct((rows, width), BF16),
        in_specs=[SMEM] + [VMEM] * 12 + [VMEM, VMEM, ANYWHERE, VMEM, SMEM, SMEM],
        out_specs=VMEM,
        scratch_shapes=edge_scratch(rows, slots, rows + ghosts.shape[0] * ghosts.shape[1], width)
        + [
            pltpu.VMEM(ghosts.shape, BF16),
            pltpu.VMEM((2 * rows, HALF), F32),
            pltpu.SemaphoreType.DMA((ghosts.shape[0],)),
        ],
        compiler_params=pltpu.CompilerParams(vmem_limit_bytes=VMEM_BYTES),
        name="last_step",
    )(*layer_args, table, projected, ghosts, living, place_ids, count)


def pick_rows(source_rows, row_ids):
    selector = (
        row_ids[:, None] == jnp.arange(source_rows.shape[0], dtype=jnp.int32)[None, :]
    ).astype(source_rows.dtype)
    return jnp.dot(selector, source_rows, preferred_element_type=F32).astype(source_rows.dtype)


def local(
    latent,
    live_count,
    leave_rows,
    leave_target,
    halo_rows,
    neighbours,
    edge_in,
    edge_bias,
    edge_out,
    edge_shift,
    edge_gain,
    node_in,
    node_bias,
    node_out,
    node_shift,
    node_gain,
):
    axes = ("gx", "gy", "gz")
    devices = lax.axis_size(axes)
    local_rows, width = latent.shape
    table_rows, slots = neighbours.shape
    slots_total = table_rows - local_rows
    capacity = slots_total // devices
    leaving = leave_rows.shape[0]
    target_domain = leave_target[:, 0]
    entry = jnp.arange(leaving, dtype=jnp.int32)
    earlier = entry[None, :] < entry[:, None]
    same_target = target_domain[:, None] == target_domain[None, :]
    row_rank = jnp.sum(jnp.logical_and(same_target, earlier).astype(jnp.int32), axis=1)
    position = target_domain * capacity + row_rank
    moving = pick_rows(latent, leave_rows)
    moving = jnp.concatenate([moving, jnp.ones((leaving, HALF), BF16)], axis=1)
    placement = jnp.arange(slots_total, dtype=jnp.int32)[:, None] == position[None, :]
    outgoing = jnp.dot(placement.astype(BF16), moving, preferred_element_type=F32).astype(BF16)
    arrived = lax.all_to_all(
        outgoing.reshape(devices, capacity, width + HALF), axes, split_axis=0, concat_axis=0, tiled=True
    ).reshape(slots_total, width + HALF)
    local_index = jnp.arange(local_rows, dtype=jnp.int32)
    departed = jnp.any(local_index[:, None] == leave_rows[None, :], axis=1)
    local_live = jnp.logical_and(local_index < live_count[0], jnp.logical_not(departed)).astype(F32)
    living = jnp.concatenate([local_live[:, None], arrived[:, width : width + 1].astype(F32)], axis=0)

    edge_ids, floor, order, place_ids, count = order_rows(neighbours, halo_rows)
    place_ids = place_ids.reshape(-1)
    order = order.reshape(-1)
    table, projected, boundary = open_table(latent, arrived[:, :width], 2 * halo_rows, order, edge_in[0, 1])
    blocks = (local_rows - leaving + slots_total) // ROWS

    def layer_args(t):
        return (
            edge_ids,
            floor,
            edge_in[t, 0],
            edge_bias[t][None],
            edge_out[t],
            edge_shift[t][None],
            edge_gain[t][None],
            node_in[t, 0],
            node_in[t, 1],
            node_bias[t][None],
            node_out[t],
            node_shift[t][None],
            node_gain[t][None],
        )

    table, projected, ghosts = first_step(blocks, layer_args(0), table, projected, boundary, edge_in[1, 1])
    return last_step(layer_args(1), table, projected, ghosts, living, place_ids, count)


def solution(mesh):
    rows = P(("gx", "gy", "gz"))
    in_specs = (rows,) * 6 + (P(),) * 10
    return jax.shard_map(local, mesh=mesh, in_specs=in_specs, out_specs=rows, check_vma=False)
```

time: 355 us -> 199 us (0.56); the launches traced: 348 us -> 199 us
  waiting for transfers between devices: 102 us -> 0.01 us
  starting transfers between devices: 42 us -> 10.3 us
  other arithmetic: 22.2 us -> 8.73 us
    ppermute x12 -> x0, waiting for transfers between devices: 95.9 us -> none  [the longest x6 79.2 us: with_halo(): before = lax.ppermute(last, axis, up)]
    ppermute x12 -> x0, starting transfers between devices: 31.7 us -> none  [the longest x6 16.5 us: with_halo(): after = lax.ppermute(first, axis, down)]
    concatenate x6 -> x1, other arithmetic: 16.1 us -> 0.74 us  [order_rows(): digits = jnp.concatenate([ids // 128, ids % 128]).astype(BF16)]
    all_to_all x1, waiting for transfers between devices: 6.16 us -> 0.01 us  [local(): lax.all_to_all(outgoing.reshape(devices, capacity, width + HALF), axes, s...]
    pallas_call x0 -> x2, other arithmetic: none -> 3.57 us  [order_rows(): pl.pallas_call(order_kernel, out_shape=(jax.ShapeDtypeStruct((slots, rows...]
    pallas_call x2 -> x3, Pallas kernels: 166 us -> 164 us  [the longest x1 92.7 us: first_step(): pl.pallas_call(functools.partial(first_step_kernel, slots, blocks, marks)...]
  transfers between devices with their start and end apart: 13 -> 1, of which waited for: 13 -> 0; matrix products, arithmetic and copies ran while one was open for 3% -> 6% of each run, Pallas kernels for 0% -> 5%
where the time goes in v3:
time: 199 us
  Pallas kernels  171 us (86%)
  starting transfers between devices  10.3 us (5%)
  other arithmetic  8.73 us (4%)
  local copies, waits for them, and re-layouts  6.74 us (3%)
    pallas_call x1, Pallas kernels, first_step(): pl.pallas_call(functools.partial(first_step_kernel, slots, blocks, marks)...  92.7 us
    pallas_call x1, Pallas kernels, last_step(): pl.pallas_call(functools.partial(last_step_kernel, slots), out_shape=jax....  60.9 us
    all_to_all x1, starting transfers between devices, local(): lax.all_to_all(outgoing.reshape(devices, capacity, width + HALF), axes, s...  10.3 us
    pallas_call x1, Pallas kernels, order_rows(): pl.pallas_call(order_kernel, out_shape=(jax.ShapeDtypeStruct((slots, rows...  10.3 us
    pallas_call x1, Pallas kernels, open_table(): pl.pallas_call(open_kernel, out_shape=(jax.ShapeDtypeStruct((rows, width)...  6.79 us
  transfers between devices with their start and end apart: 1, of which 0 were waited for; matrix products, arithmetic and copies ran while one was open for 6% of the time, Pallas kernels for 5%

profile of v3, /device:TPU:18, one launch (start us, length us, event | category | flops | bytes accessed | tf_op | source)
XLA Modules:
  0.0 199.1 jit_solution(16917154418502512254)
XLA Ops:
  0.0 0.9 convert_reduce_fusion
  0.9 0.7 multiply_add_fusion
  1.6 1.6 convolution_convert_fusion.1
  3.4 0.8 reshape.44
  4.2 10.3 %all-to-all-start = ((bf16[128,2,384]{2,1,0:T(2,128)(2,1)}), bf16[128,2,384]{2,1,0:T(2,128)(2,1)S(1)}, u32[]{:S(2)}, u32[]{:S(2)}) async-start(bf16[128,2,384]{2,1,0:T(2,128)(2,1)} %reshape.44), calls=%async_computation | async-start | bytes 393216 | tf_op jit(solution)/shard_map/all_to_all | solution.py:654
  14.5 0.4 fusion.2
  14.9 1.4 copy.25.neighbours
  17.0 0.4 fusion.4
  17.4 0.7 pad_maximum_fusion.1.digits
  18.2 10.3 %order_rows.1 = (s32[24,2304]{1,0:T(8,128)}, f32[2304,128]{1,0:T(8,128)}, s32[1,2304]{1,0:T(1,128)}, s32[2304,1]{1,0:T(8,128)}, s32[1]{0:T(128)}) custom-call(s32[2304,24]{1,0:T(8,128)} %copy.25.neighbours, bf16[64,2304]{1,0:T(8,128)(2,1)} %pad_maximum_fusion.1.digits, s32[1,512]{1,0:T(1,128)} %bitcast.32), custom_call_target="tpu_custom_call" | custom-call | tf_op jit(solution)/shard_map/order_rows/pallas_call | solution.py:119
  28.5 1.3 reduce.order
  29.8 2.3 %reduce.1.args_17_ = s32[2304]{0:T(1024)} reduce(s32[2304,1]{1,0:T(8,128)} %get-tuple-element.25, s32[]{:T(128)} %constant.30.clone.1), dimensions={1}, to_apply=%get-tuple-element.25.reduce_sub_computation | reduce | bytes 18436 | tf_op jit(solution)/shard_map/order_rows/pallas_call | solution.py:119
  32.1 0.6 fusion.16
  32.7 0.6 fusion.14
  33.3 0.6 fusion.12
  33.9 0.8 slice_bitcast_fusion.2
  34.7 0.3 fusion.1
  35.1 1.1 slice_bitcast_fusion
  36.2 0.6 broadcast_multiply_fusion.halo_ids
  36.8 0.7 slice.104.arrived_ref
  37.5 1.2 pad_maximum_fusion.args_16_
  38.7 6.8 %open_table.1 = (bf16[2304,256]{1,0:T(8,128)(2,1)}, bf16[2304,256]{1,0:T(8,128)(2,1)}, bf16[512,256]{1,0:T(8,128)(2,1)}) custom-call(bf16[2048,256]{1,0:T(8,128)(2,1)} %latent_ref.1, bf16[256,256]{1,0:T(8,128)(2,1)} %slice.104.arrived_ref, s32[512]{0:T(512)} %broadcast_multiply_fusion.halo_ids, s32[2304]{0:T(1024)} %reduce.order, ...), custom_call_target="tpu_custom_call" | custom-call | tf_op jit(solution)/shard_map/open_table/pallas_call | solution.py:171
  45.5 92.7 %first_step.1 = (bf16[2304,256]{1,0:T(8,128)(2,1)}, bf16[2304,256]{1,0:T(8,128)(2,1)}, bf16[27,512,256]{2,1,0:T(8,128)(2,1)}) custom-call(s32[24,2304]{1,0:T(8,128)} %get-tuple-element.16.args_0_, f32[2304,128]{1,0:T(8,128)} %get-tuple-element.17.args_1_, bf16[256,256]{1,0:T(8,128)(2,1)} %get-tuple-element.28.args_2_, f32[1,256]{1,0:T(1,128)} %get-tuple-element.64.args_3_, ...), custom_call_target="tpu_custom_call" | custom-call | tf_op jit(solution)/shard_map/first_step/pallas_call | solution.py:513
  138.2 60.9 %last_step.1 = bf16[2304,256]{1,0:T(8,128)(2,1)} custom-call(s32[24,2304]{1,0:T(8,128)} %get-tuple-element.16.args_0_, f32[2304,128]{1,0:T(8,128)} %get-tuple-element.17.args_1_, bf16[256,256]{1,0:T(8,128)(2,1)} %get-tuple-element.29.args_2_, f32[1,256]{1,0:T(1,128)} %get-tuple-element.63.args_3_, bf16[256,256]{1,0:T(8,128)(2,1)} %get-tuple-element.57.args_4_, ...), custom_call_target="tpu_custom_call" | custom-call | tf_op jit(solution)/shard_map/last_step/pallas_call | solution.py:596
  (35 shorter events, 0.5 us)
Async XLA Ops:
  0.0 14.5 %copy-start.12 = (s32[128]{0:T(128)S(1)}, s32[128]{0:T(128)}, u32[]{:S(2)}) copy-start(s32[128]{0:T(128)} %param.18) | copy-start | bytes 1540
  0.0 14.8 %copy-start = (s32[2304,24]{0,1:T(8,128)S(1)}, s32[2304,24]{0,1:T(8,128)}, u32[]{:S(2)}) copy-start(s32[2304,24]{0,1:T(8,128)} %param.21) | copy-start | bytes 663556
  4.2 32.6 %all-to-all-start = ((bf16[128,2,384]{2,1,0:T(2,128)(2,1)}), bf16[128,2,384]{2,1,0:T(2,128)(2,1)S(1)}, u32[]{:S(2)}, u32[]{:S(2)}) async-start(bf16[128,2,384]{2,1,0:T(2,128)(2,1)} %reshape.44), calls=%async_computation | async-start | bytes 393216 | tf_op jit(solution)/shard_map/all_to_all | solution.py:654
  18.1 13.9 %copy-start.6 = (f32[2,256]{1,0:T(2,128)S(1)}, f32[2,256]{1,0:T(2,128)}, u32[]{:S(2)}) copy-start(f32[2,256]{1,0:T(2,128)} %param.25) | copy-start | bytes 6148
  18.1 13.9 %copy-start.7 = (f32[2,256]{1,0:T(2,128)S(1)}, f32[2,256]{1,0:T(2,128)}, u32[]{:S(2)}) copy-start(f32[2,256]{1,0:T(2,128)} %param.23) | copy-start | bytes 6148
  18.1 14.5 %copy-start.8 = (f32[2,256]{1,0:T(2,128)S(1)}, f32[2,256]{1,0:T(2,128)}, u32[]{:S(2)}) copy-start(f32[2,256]{1,0:T(2,128)} %param.28) | copy-start | bytes 6148
  18.1 14.5 %copy-start.9 = (f32[2,256]{1,0:T(2,128)S(1)}, f32[2,256]{1,0:T(2,128)}, u32[]{:S(2)}) copy-start(f32[2,256]{1,0:T(2,128)} %param.26) | copy-start | bytes 6148
  18.1 15.2 %copy-start.10 = (f32[2,256]{1,0:T(2,128)S(1)}, f32[2,256]{1,0:T(2,128)}, u32[]{:S(2)}) copy-start(f32[2,256]{1,0:T(2,128)} %param.31) | copy-start | bytes 6148
  18.1 15.1 %copy-start.11 = (f32[2,256]{1,0:T(2,128)S(1)}, f32[2,256]{1,0:T(2,128)}, u32[]{:S(2)}) copy-start(f32[2,256]{1,0:T(2,128)} %param.30) | copy-start | bytes 6148
  18.1 15.7 %copy-start.3 = (bf16[2,256,256]{2,1,0:T(8,128)(2,1)S(1)}, bf16[2,256,256]{2,1,0:T(8,128)(2,1)}, u32[]{:S(2)}) copy-start(bf16[2,256,256]{2,1,0:T(8,128)(2,1)} %param.29) | copy-start | bytes 786436
  18.2 15.7 %copy-start.4 = (bf16[2,256,256]{2,1,0:T(8,128)(2,1)S(1)}, bf16[2,256,256]{2,1,0:T(8,128)(2,1)}, u32[]{:S(2)}) copy-start(bf16[2,256,256]{2,1,0:T(8,128)(2,1)} %param.24) | copy-start | bytes 786436
  32.1 3.0 %copy-start.1 = (bf16[2,2,256,256]{3,2,1,0:T(8,128)(2,1)S(1)}, bf16[2,2,256,256]{3,2,1,0:T(8,128)(2,1)}, u32[]{:S(2)}) copy-start(bf16[2,2,256,256]{3,2,1,0:T(8,128)(2,1)} %param.22) | copy-start | bytes 1572868
  32.1 3.0 %copy-start.2 = (bf16[2,2,256,256]{3,2,1,0:T(8,128)(2,1)S(1)}, bf16[2,2,256,256]{3,2,1,0:T(8,128)(2,1)}, u32[]{:S(2)}) copy-start(bf16[2,2,256,256]{3,2,1,0:T(8,128)(2,1)} %param.27) | copy-start | bytes 1572868
  35.1 1.1 copy-start.5

commit v4 on v3

--- a/solution.py
+++ b/solution.py
@@ -13,8 +13,10 @@
 HALF = 128
 ROWS = 32
 CHUNK = 256
+LAG = 2
 GROUP = 8
 NODE_ROWS = 256
+SPARE = 8
 AXES = ("gx", "gy", "gz")
 MESH = pl.DeviceIdType.MESH
 VMEM_BYTES = 58 * 2**20
@@ -52,13 +54,14 @@
         for g in range(64 // GROUP):
             some = ids.at[pl.ds(block * 64 + g * GROUP, GROUP)]
             for e in range(GROUP):
-                row = pl.multiple_of(some[e], 2)
                 place = pl.multiple_of(2 * (block * 64 + g * GROUP + e), 2)
-                into[pl.ds(place, 2), :] = source[pl.ds(row, 2), :]
-
-
-def order_kernel(neighbours, digits, halo_lanes, edge_ids, floor_ref, order_ref, place_ref, count_ref, places):
-    rows, slots = neighbours.shape
+                into[pl.ds(place, 2), :] = source[pl.ds(2 * some[e], 2), :]
+
+
+def find_places(digits, halo_lanes, places, place_ref, count_ref):
+    rows = digits.shape[1]
+    half_rows = digits.shape[0] // 2
+    slots = half_rows - SPARE
     boundary = halo_lanes.shape[1]
     n = NODE_ROWS
     lower = (
@@ -69,118 +72,64 @@
     def one_chunk(c, carry):
         used, spare = carry
         first = pl.multiple_of(c * n, n)
-        active = jnp.max(neighbours[pl.ds(first, n), :], axis=1, keepdims=True) >= 0
+        here = pl.ds(first, n)
+        largest = jnp.max(
+            digits[pl.ds(0, slots), here].astype(F32) + digits[pl.ds(half_rows, slots), here].astype(F32),
+            axis=0,
+            keepdims=True,
+        )
+        active = jnp.transpose(jnp.broadcast_to(largest, (HALF, n))) > 0.0
         row_ids = lax.broadcasted_iota(jnp.int32, (n, boundary), 0) + first
         same = (row_ids == halo_lanes[...]).astype(F32)
         listed = jnp.sum(same, axis=1, keepdims=True) > 0.0
         position = jnp.sum(same * lane, axis=1, keepdims=True)
         others = jnp.where(listed, 0.0, jnp.where(active, 1.0, 0.0))
         idle = jnp.where(listed, 0.0, jnp.where(active, 0.0, 1.0))
-        others = jnp.broadcast_to(others, (n, HALF))
-        idle = jnp.broadcast_to(idle, (n, HALF))
         before = jnp.dot(lower, others.astype(BF16), preferred_element_type=F32) + used
         behind = jnp.dot(lower, idle.astype(BF16), preferred_element_type=F32) + spare
         place = jnp.where(others > 0.0, boundary + before, rows - 1 - behind)
         place = jnp.where(listed, position, place)
-        places[pl.ds(first, n), :] = place
-        place_ref[pl.ds(first, n), :] = (2.0 * place[:, :1]).astype(jnp.int32)
+        places[here, :] = place
+        place_ref[:, here] = jnp.transpose(place)[:1].astype(jnp.int32)
         return used + jnp.sum(others[:, :1]), spare + jnp.sum(idle[:, :1])
 
     used, _ = lax.fori_loop(0, rows // n, one_chunk, (jnp.float32(0.0), jnp.float32(0.0)))
     count_ref[0] = used.astype(jnp.int32) + boundary
+
+
+def apply_places(senders, digits, places, edge_ids, floor_ref, order_ref):
+    rows = digits.shape[1]
+    half_rows = digits.shape[0] // 2
+    slots = half_rows - SPARE
+    n = NODE_ROWS
 
     @pl.loop(0, rows // n)
     def _(c):
         first = pl.multiple_of(c * n, n)
-        halves = []
-        for half in range(n // HALF):
-            lanes = lax.broadcasted_iota(jnp.int32, (rows, HALF), 1).astype(F32)
-            wanted = lanes + (first + half * HALF).astype(F32)
-            halves.append(jnp.where(places[...] == wanted, 1.0, 0.0).astype(BF16))
-        chosen = jnp.concatenate(halves, axis=1)
-        picked = jnp.dot(digits[...], chosen, preferred_element_type=F32)
-        half_rows = digits.shape[0] // 2
+        lanes = lax.broadcasted_iota(jnp.int32, (n, HALF), 1).astype(F32)
+        picked = jnp.zeros((2 * half_rows, n), F32)
+        for part in range(rows // n):
+            here = places[pl.ds(part * n, n), :]
+            halves = [
+                jnp.where(here == lanes + (first + half * HALF).astype(F32), 1.0, 0.0).astype(BF16)
+                for half in range(n // HALF)
+            ]
+            chosen = jnp.concatenate(halves, axis=1)
+            picked = picked + jnp.dot(digits[:, pl.ds(part * n, n)], chosen, preferred_element_type=F32)
         value = picked[:half_rows] * 128.0 + picked[half_rows:]
         here = pl.ds(first, n)
-        edge_ids[:, here] = (2.0 * jnp.maximum(value[:slots] - 1.0, 0.0)).astype(jnp.int32)
-        order_ref[:, here] = (2.0 * value[slots : slots + 1]).astype(jnp.int32)
+        edge_ids[:, here] = 2 * jnp.clip((value[:slots] - 1.0).astype(jnp.int32), 0, senders - 1)
+        order_ref[:, here] = jnp.clip(value[slots : slots + 1].astype(jnp.int32), 0, rows - 1)
         floor = jnp.where(value > 0.5, EPS, jnp.inf).astype(F32)
         floor_ref[here, :] = jnp.transpose(jnp.concatenate([floor] * (HALF // half_rows), axis=0))
 
 
-def order_rows(neighbours, halo_rows):
+def digits_of(neighbours):
     rows, slots = neighbours.shape
-    half_rows = 32
-    ids = neighbours.T + 1
     ids = jnp.concatenate(
-        [ids, jnp.arange(rows, dtype=jnp.int32)[None], jnp.zeros((half_rows - slots - 1, rows), jnp.int32)]
+        [neighbours.T + 1, jnp.arange(rows, dtype=jnp.int32)[None], jnp.zeros((SPARE - 1, rows), jnp.int32)]
     )
-    digits = jnp.concatenate([ids // 128, ids % 128]).astype(BF16)
-    return pl.pallas_call(
-        order_kernel,
-        out_shape=(
-            jax.ShapeDtypeStruct((slots, rows), jnp.int32),
-            jax.ShapeDtypeStruct((rows, HALF), F32),
-            jax.ShapeDtypeStruct((1, rows), jnp.int32),
-            jax.ShapeDtypeStruct((rows, 1), jnp.int32),
-            jax.ShapeDtypeStruct((1,), jnp.int32),
-        ),
-        in_specs=[VMEM, VMEM, VMEM],
-        out_specs=(VMEM, VMEM, VMEM, VMEM, SMEM),
-        scratch_shapes=[pltpu.VMEM((rows, HALF), F32)],
-        compiler_params=pltpu.CompilerParams(vmem_limit_bytes=VMEM_BYTES),
-        name="order_rows",
-    )(neighbours, digits, halo_rows[None, :])
-
-
-def open_kernel(latent_ref, arrived_ref, halo_ids, order, weight_ref, ordered_ref, projected_ref, boundary_ref, pairs, picked):
-    local_rows = latent_ref.shape[0]
-    arrivals = arrived_ref.shape[0]
-    rows = local_rows + arrivals
-
-    def sources(take):
-        @pl.loop(0, local_rows // NODE_ROWS)
-        def _(i):
-            first = pl.multiple_of(i * NODE_ROWS, NODE_ROWS)
-            take(first, latent_ref[pl.ds(first, NODE_ROWS), :])
-
-        take(local_rows, arrived_ref[...])
-
-    def projection(first, values):
-        projected = project(values, weight_ref[...])
-        projected_ref[pl.ds(first, NODE_ROWS), :] = projected
-        store_split(pairs, first, projected.astype(F32))
-
-    sources(projection)
-    count = boundary_ref.shape[0]
-    copy_rows(pairs, halo_ids, picked, count)
-    boundary_ref[...] = load_split(picked, 0, count).astype(BF16)
-    sources(lambda first, values: store_split(pairs, first, values.astype(F32)))
-    copy_rows(pairs, order, picked, rows)
-
-    @pl.loop(0, rows // NODE_ROWS)
-    def _(i):
-        first = pl.multiple_of(i * NODE_ROWS, NODE_ROWS)
-        ordered_ref[pl.ds(first, NODE_ROWS), :] = load_split(picked, first, NODE_ROWS).astype(BF16)
-
-
-def open_table(latent, arrived, halo_ids, order, weight):
-    rows = latent.shape[0] + arrived.shape[0]
-    width = latent.shape[1]
-    count = halo_ids.shape[0]
-    return pl.pallas_call(
-        open_kernel,
-        out_shape=(
-            jax.ShapeDtypeStruct((rows, width), BF16),
-            jax.ShapeDtypeStruct((rows, width), BF16),
-            jax.ShapeDtypeStruct((count, width), BF16),
-        ),
-        in_specs=[VMEM, VMEM, SMEM, SMEM, VMEM],
-        out_specs=(VMEM, VMEM, VMEM),
-        scratch_shapes=[pltpu.VMEM((2 * rows, HALF), F32), pltpu.VMEM((2 * rows, HALF), F32)],
-        compiler_params=pltpu.CompilerParams(vmem_limit_bytes=VMEM_BYTES),
-        name="open_table",
-    )(latent, arrived, halo_ids, order, weight)
+    return jnp.concatenate([ids // 128, ids % 128]).astype(BF16)
 
 
 class Grid:
@@ -347,12 +296,12 @@
         shift = edge_shift[...] - jnp.mean(edge_shift[...], axis=1, keepdims=True)
         floor = self.floor[pl.ds(first, ROWS), :]
         sums = (jnp.zeros((ROWS, HALF), F32), jnp.zeros((ROWS, HALF), F32))
-        for chunk in range(chunks + 1):
+        for chunk in range(chunks + LAG):
             if chunk < chunks:
                 self.gather(self.buffers[1 - parity], following, chunk * CHUNK, (chunk + 1) * CHUNK)
                 self.first_half(self.buffers[parity], first, chunk, shift)
-            if chunk > 0:
-                sums = self.second_half(floor, chunk - 1, sums)
+            if chunk >= LAG:
+                sums = self.second_half(floor, chunk - LAG, sums)
         self.summed[pl.ds(first, ROWS), :HALF] = sums[0]
         self.summed[pl.ds(first, ROWS), HALF:] = sums[1]
 
@@ -370,21 +319,24 @@
     return own.astype(F32) + layer_norm(node_raw, refs["node_gain"][...])
 
 
-NAMES = (
-    "edge_ids",
-    "floor",
-    "receive_weight",
-    "edge_bias",
-    "edge_out",
-    "edge_shift",
-    "edge_gain",
-    "node_self",
-    "node_message",
-    "node_bias",
-    "node_out",
-    "node_shift",
-    "node_gain",
-)
+def step_refs(t, edge_ids, floor, weights):
+    edge_in, edge_bias, edge_out, edge_shift, edge_gain, node_in, node_bias, node_out, node_shift, node_gain = weights
+    row = pl.ds(t, 1)
+    return {
+        "edge_ids": edge_ids,
+        "floor": floor,
+        "receive_weight": edge_in.at[t, 0],
+        "edge_bias": edge_bias.at[row],
+        "edge_out": edge_out.at[t],
+        "edge_shift": edge_shift.at[row],
+        "edge_gain": edge_gain.at[row],
+        "node_self": node_in.at[t, 0],
+        "node_message": node_in.at[t, 1],
+        "node_bias": node_bias.at[row],
+        "node_out": node_out.at[t],
+        "node_shift": node_shift.at[row],
+        "node_gain": node_gain.at[row],
+    }
 
 
 def edge_scratch(rows, slots, senders, width):
@@ -414,42 +366,86 @@
 
 
 def first_step_kernel(slots, blocks, marks, *args):
-    refs = dict(zip(NAMES, args))
-    table_ref, projected_ref, boundary_ref, next_weight = args[13:17]
-    renewed_ref, next_projected, next_ghosts = args[17:20]
-    scratch = unpack_scratch(args[20:28])
-    ghosts, next_boundary, send_a, recv_a, send_b, recv_b = args[28:]
+    latent_ref, arrived_ref, digits, halo_lanes, halo_ids = args[:5]
+    weights = args[5:15]
+    renewed_ref, next_projected, next_ghosts, edge_lanes, floor_ref, place_ref, count_ref = args[15:22]
+    scratch = unpack_scratch(args[22:30])
+    (
+        ghosts,
+        boundary_ref,
+        next_boundary,
+        original,
+        ordered,
+        places,
+        table_ref,
+        order_lanes,
+        edge_ids,
+        order_ids,
+        send_a,
+        recv_a,
+        send_b,
+        recv_b,
+        id_sems,
+    ) = args[30:]
     pairs, summed = scratch[0], scratch[3]
-    rows = table_ref.shape[0]
+    local_rows, width = latent_ref.shape
+    arrivals = arrived_ref.shape[0]
+    rows = local_rows + arrivals
     boundary_rows = boundary_ref.shape[0]
+    refs = step_refs(0, edge_ids, floor_ref, weights)
+    send_weight, next_weight = weights[0].at[0, 1], weights[0].at[1, 1]
     grid = Grid()
     now = Exchange(grid, boundary_ref, ghosts, send_a, recv_a)
     later = Exchange(grid, next_boundary, next_ghosts, send_b, recv_b)
     layers = EdgeLayers(rows, slots, refs, scratch)
     grid.greet()
+
+    def take(first, values):
+        store_split(original, first, values.astype(F32))
+        store_split(pairs, first, project(values, send_weight[...]).astype(F32))
+
+    @pl.loop(0, local_rows // NODE_ROWS)
+    def _(i):
+        first = pl.multiple_of(i * NODE_ROWS, NODE_ROWS)
+        take(first, latent_ref[pl.ds(first, NODE_ROWS), :])
+
+    for first in range(0, arrivals, NODE_ROWS):
+        take(local_rows + first, arrived_ref[pl.ds(first, NODE_ROWS), :width])
+    copy_rows(pairs, halo_ids, ordered, boundary_rows)
+    boundary_ref[...] = load_split(ordered, 0, boundary_rows).astype(BF16)
     now.forward(CENTRE)
-    layers.prepare(table_ref)
+    find_places(digits, halo_lanes, places, place_ref, count_ref)
+
+    def spread(offset):
+        spread_block(pairs, rows + number(offset) * boundary_rows, ghosts.at[number(offset)])
+
+    def spread_all(offsets):
+        for offset in offsets:
+
+            @pl.when(grid.present(offset))
+            def _():
+                spread(offset)
+
+    now.relay(MIDDLE)
+    now.relay(SIDES[:2])
+    apply_places(pairs.shape[0] // 2, digits, places, edge_lanes, floor_ref, order_lanes)
+    fetch_edges = pltpu.make_async_copy(edge_lanes, edge_ids, id_sems.at[0])
+    fetch_order = pltpu.make_async_copy(order_lanes, order_ids, id_sems.at[1])
+    fetch_edges.start()
+    fetch_order.start()
+    spread_all(MIDDLE)
+    spread_all(SIDES[:2])
+    now.relay(SIDES[2:])
+    fetch_edges.wait()
+    fetch_order.wait()
+    copy_rows(original, order_ids.at[0], ordered, rows)
 
     @pl.loop(0, rows // NODE_ROWS)
     def _(i):
         first = pl.multiple_of(i * NODE_ROWS, NODE_ROWS)
-        store_split(pairs, first, projected_ref[pl.ds(first, NODE_ROWS), :].astype(F32))
-
-    def spread(offset):
-        spread_block(pairs, rows + number(offset) * boundary_rows, ghosts.at[number(offset)])
-
-    def spread_all(offsets):
-        for offset in offsets:
-
-            @pl.when(grid.present(offset))
-            def _():
-                spread(offset)
-
-    now.relay(MIDDLE)
-    now.relay(SIDES[:2])
-    spread_all(MIDDLE)
-    spread_all(SIDES[:2])
-    now.relay(SIDES[2:])
+        table_ref[pl.ds(first, NODE_ROWS), :] = load_split(ordered, first, NODE_ROWS).astype(BF16)
+
+    layers.prepare(table_ref)
     spread_all(SIDES[2:])
     for offset in ENDS:
 
@@ -503,10 +499,11 @@
     later.finish_sends()
 
 
-def first_step(blocks, layer_args, table, projected, boundary, next_weight):
-    rows, width = table.shape
-    slots = layer_args[0].shape[0]
-    count = boundary.shape[0]
+def first_step(blocks, latent, arrived, digits, halo_rows, weights):
+    local_rows, width = latent.shape
+    rows = local_rows + arrived.shape[0]
+    slots = digits.shape[0] // 2 - SPARE
+    count = halo_rows.shape[0]
     first_pair = count // ROWS // 2
     rest = blocks // 2 - first_pair
     marks = (first_pair, first_pair + rest * 5 // 26, first_pair + rest * 7 // 26, first_pair + rest * 14 // 26)
@@ -516,27 +513,46 @@
             jax.ShapeDtypeStruct((rows, width), BF16),
             jax.ShapeDtypeStruct((rows, width), BF16),
             jax.ShapeDtypeStruct((27, count, width), BF16),
+            jax.ShapeDtypeStruct((slots, rows), jnp.int32),
+            jax.ShapeDtypeStruct((rows, HALF), F32),
+            jax.ShapeDtypeStruct((1, rows), jnp.int32),
+            jax.ShapeDtypeStruct((1,), jnp.int32),
         ),
-        in_specs=[SMEM] + [VMEM] * 16,
-        out_specs=(VMEM, VMEM, ANYWHERE),
+        in_specs=[VMEM] * 4 + [SMEM] + [VMEM] * 10,
+        out_specs=(VMEM, VMEM, ANYWHERE, VMEM, VMEM, VMEM, SMEM),
         scratch_shapes=edge_scratch(rows, slots, rows + 27 * count, width)
-        + [pltpu.VMEM((27, count, width), BF16), pltpu.VMEM((count, width), BF16)]
-        + [pltpu.SemaphoreType.DMA((27,))] * 4,
+        + [
+            pltpu.VMEM((27, count, width), BF16),
+            pltpu.VMEM((count, width), BF16),
+            pltpu.VMEM((count, width), BF16),
+            pltpu.VMEM((2 * rows, HALF), F32),
+            pltpu.VMEM((2 * rows, HALF), F32),
+            pltpu.VMEM((rows, HALF), F32),
+            pltpu.VMEM((rows, width), BF16),
+            pltpu.VMEM((1, rows), jnp.int32),
+            pltpu.SMEM((slots, rows), jnp.int32),
+            pltpu.SMEM((1, rows), jnp.int32),
+        ]
+        + [pltpu.SemaphoreType.DMA((27,))] * 4
+        + [pltpu.SemaphoreType.DMA((2,))],
         compiler_params=pltpu.CompilerParams(
             collective_id=0, has_side_effects=True, vmem_limit_bytes=VMEM_BYTES
         ),
         name="first_step",
-    )(*layer_args, table, projected, boundary, next_weight)
+    )(latent, arrived, digits, halo_rows[None, :], halo_rows, *weights)
 
 
 def last_step_kernel(slots, *args):
-    refs = dict(zip(NAMES, args))
-    table_ref, projected_ref, ghosts, living_ref, place_ids, count_ref = args[13:19]
-    updated_ref = args[19]
-    scratch = unpack_scratch(args[20:28])
-    staged, ordered, sems = args[28:]
+    edge_ids, floor_ref, table_ref, projected_ref, ghosts = args[:5]
+    place_ids, count_ref, live_count, leave_lanes, arrived_ref = args[5:10]
+    weights = args[10:20]
+    updated_ref = args[20]
+    scratch = unpack_scratch(args[21:29])
+    staged, ordered, sems = args[29:]
+    refs = step_refs(1, edge_ids, floor_ref, weights)
     pairs, summed = scratch[0], scratch[3]
-    rows = table_ref.shape[0]
+    rows, width = table_ref.shape
+    local_rows = rows - arrived_ref.shape[0]
     ghost_blocks, ghost_rows = ghosts.shape[0], ghosts.shape[1]
     centre = ghost_blocks // 2
     layers = EdgeLayers(rows, slots, refs, scratch)
@@ -554,7 +570,7 @@
         first = pl.multiple_of(i * NODE_ROWS, NODE_ROWS)
         store_split(ordered, first, projected_ref[pl.ds(first, NODE_ROWS), :].astype(F32))
 
-    copy_rows(ordered, place_ids, pairs, rows)
+    copy_rows(ordered, place_ids.at[0], pairs, rows)
 
     @pl.loop(0, ghost_blocks)
     def _(block):
@@ -581,22 +597,30 @@
         renewed = node_layers(refs, table_ref, summed, pl.ds(first, NODE_ROWS))
         store_split(ordered, first, renewed)
 
-    copy_rows(ordered, place_ids, pairs, rows)
-
-    @pl.loop(0, rows // NODE_ROWS)
+    copy_rows(ordered, place_ids.at[0], pairs, rows)
+
+    @pl.loop(0, local_rows // NODE_ROWS)
     def _(i):
         first = pl.multiple_of(i * NODE_ROWS, NODE_ROWS)
-        here = pl.ds(first, NODE_ROWS)
-        updated_ref[here, :] = (load_split(pairs, first, NODE_ROWS) * living_ref[here, :]).astype(BF16)
-
-
-def last_step(layer_args, table, projected, ghosts, living, place_ids, count):
+        row_ids = lax.broadcasted_iota(jnp.int32, (NODE_ROWS, leave_lanes.shape[1]), 0) + first
+        leaves = jnp.max((row_ids == leave_lanes[...]).astype(F32), axis=1, keepdims=True)
+        living = jnp.where(row_ids[:, :1] < live_count[0], 1.0 - leaves, 0.0)
+        updated_ref[pl.ds(first, NODE_ROWS), :] = (load_split(pairs, first, NODE_ROWS) * living).astype(BF16)
+
+    for first in range(0, rows - local_rows, NODE_ROWS):
+        living = arrived_ref[pl.ds(first, NODE_ROWS), width : width + 1].astype(F32)
+        updated_ref[pl.ds(local_rows + first, NODE_ROWS), :] = (
+            load_split(pairs, local_rows + first, NODE_ROWS) * living
+        ).astype(BF16)
+
+
+def last_step(edge_ids, floor, table, projected, ghosts, place_ids, count, live_count, leave_rows, arrived, weights):
     rows, width = table.shape
-    slots = layer_args[0].shape[0]
+    slots = edge_ids.shape[0]
     return pl.pallas_call(
         functools.partial(last_step_kernel, slots),
         out_shape=jax.ShapeDtypeStruct((rows, width), BF16),
-        in_specs=[SMEM] + [VMEM] * 12 + [VMEM, VMEM, ANYWHERE, VMEM, SMEM, SMEM],
+        in_specs=[SMEM, VMEM, VMEM, VMEM, ANYWHERE, SMEM, SMEM, SMEM] + [VMEM] * 12,
         out_specs=VMEM,
         scratch_shapes=edge_scratch(rows, slots, rows + ghosts.shape[0] * ghosts.shape[1], width)
         + [
@@ -606,7 +630,19 @@
         ],
         compiler_params=pltpu.CompilerParams(vmem_limit_bytes=VMEM_BYTES),
         name="last_step",
-    )(*layer_args, table, projected, ghosts, living, place_ids, count)
+    )(
+        edge_ids,
+        floor,
+        table,
+        projected,
+        ghosts,
+        place_ids,
+        count,
+        live_count,
+        leave_rows[None, :],
+        arrived,
+        *weights,
+    )
 
 
 def pick_rows(source_rows, row_ids):
@@ -654,36 +690,25 @@
     arrived = lax.all_to_all(
         outgoing.reshape(devices, capacity, width + HALF), axes, split_axis=0, concat_axis=0, tiled=True
     ).reshape(slots_total, width + HALF)
-    local_index = jnp.arange(local_rows, dtype=jnp.int32)
-    departed = jnp.any(local_index[:, None] == leave_rows[None, :], axis=1)
-    local_live = jnp.logical_and(local_index < live_count[0], jnp.logical_not(departed)).astype(F32)
-    living = jnp.concatenate([local_live[:, None], arrived[:, width : width + 1].astype(F32)], axis=0)
-
-    edge_ids, floor, order, place_ids, count = order_rows(neighbours, halo_rows)
-    place_ids = place_ids.reshape(-1)
-    order = order.reshape(-1)
-    table, projected, boundary = open_table(latent, arrived[:, :width], 2 * halo_rows, order, edge_in[0, 1])
+    weights = (
+        edge_in,
+        edge_bias,
+        edge_out,
+        edge_shift,
+        edge_gain,
+        node_in,
+        node_bias,
+        node_out,
+        node_shift,
+        node_gain,
+    )
     blocks = (local_rows - leaving + slots_total) // ROWS
-
-    def layer_args(t):
-        return (
-            edge_ids,
-            floor,
-            edge_in[t, 0],
-            edge_bias[t][None],
-            edge_out[t],
-            edge_shift[t][None],
-            edge_gain[t][None],
-            node_in[t, 0],
-            node_in[t, 1],
-            node_bias[t][None],
-            node_out[t],
-            node_shift[t][None],
-            node_gain[t][None],
-        )
-
-    table, projected, ghosts = first_step(blocks, layer_args(0), table, projected, boundary, edge_in[1, 1])
-    return last_step(layer_args(1), table, projected, ghosts, living, place_ids, count)
+    table, projected, ghosts, edge_ids, floor, place_ids, count = first_step(
+        blocks, latent, arrived, digits_of(neighbours), halo_rows, weights
+    )
+    return last_step(
+        edge_ids, floor, table, projected, ghosts, place_ids, count, live_count, leave_rows, arrived, weights
+    )
 
 
 def solution(mesh):

time: 199 us -> 179 us (0.90)
  Pallas kernels: 171 us -> 156 us
  other arithmetic: 8.73 us -> 2.67 us
  waiting for transfers between devices: 0.01 us -> 5.94 us
  local copies, waits for them, and re-layouts: 6.74 us -> 1.58 us
    pallas_call x2 -> x0, Pallas kernels: 17.1 us -> none  [the longest x1 10.3 us: order_rows(): pl.pallas_call(order_kernel, out_shape=(jax.ShapeDtypeStruct((slots, rows...]
    all_to_all x1, waiting for transfers between devices: 0.01 us -> 5.94 us  [local(): lax.all_to_all(outgoing.reshape(devices, capacity, width + HALF), axes, s...]
    pallas_call x2 -> x0, other arithmetic: 3.57 us -> none  [order_rows(): pl.pallas_call(order_kernel, out_shape=(jax.ShapeDtypeStruct((slots, rows...]
    slice x4 -> x0, local copies, waits for them, and re-layouts: 2.48 us -> none  [the longest x1 0.66 us: local(): arrived[:, :width]]
  transfers between devices with their start and end apart: 1 -> 1, of which waited for: 0 -> 1; matrix products, arithmetic and copies ran while one was open for 6% -> 1% of each run, Pallas kernels for 5% -> 0%
where the time goes in v4:
time: 179 us
  Pallas kernels  156 us (87%)
  starting transfers between devices  10.3 us (6%)
  waiting for transfers between devices  5.94 us (3%)
  other arithmetic  2.67 us (1%)
  matrix products  1.79 us (1%)
    pallas_call x1, Pallas kernels, first_step(): pl.pallas_call(functools.partial(first_step_kernel, slots, blocks, marks)...  94.2 us
    pallas_call x1, Pallas kernels, last_step(): pl.pallas_call(functools.partial(last_step_kernel, slots), out_shape=jax....  61.7 us
    all_to_all x1, starting transfers between devices, local(): lax.all_to_all(outgoing.reshape(devices, capacity, width + HALF), axes, s...  10.3 us
    all_to_all x1, waiting for transfers between devices, local(): lax.all_to_all(outgoing.reshape(devices, capacity, width + HALF), axes, s...  5.94 us
  transfers between devices with their start and end apart: 1, of which 1 were waited for; matrix products, arithmetic and copies ran while one was open for 1% of the time, Pallas kernels for 0%

profile of v4, /device:TPU:18, one launch (start us, length us, event | category | flops | bytes accessed | tf_op | source)
XLA Modules:
  0.0 178.9 jit_solution(14405745704698382004)
XLA Ops:
  0.0 0.0 copy-start
  0.0 0.9 convert_reduce_fusion
  0.9 0.7 multiply_add_fusion
  1.6 1.6 convolution_convert_fusion.1
  3.2 0.2 convolution_convert_fusion
  3.4 0.7 reshape.16
  4.1 10.3 %all-to-all-start = ((bf16[128,2,384]{2,1,0:T(2,128)(2,1)}), bf16[128,2,384]{2,1,0:T(2,128)(2,1)S(1)}, u32[]{:S(2)}, u32[]{:S(2)}) async-start(bf16[128,2,384]{2,1,0:T(2,128)(2,1)} %reshape.16), calls=%async_computation | async-start | bytes 393216 | tf_op jit(solution)/shard_map/all_to_all | solution.py:690
  15.1 0.1 pad.5.clone
  15.2 0.0 copy-done
  15.2 0.4 fusion.1
  15.6 0.7 pad_maximum_fusion.args_2_
  16.3 5.9 %all-to-all-done = bf16[128,2,384]{2,1,0:T(2,128)(2,1)S(1)} async-done(((bf16[128,2,384]{2,1,0:T(2,128)(2,1)}), bf16[128,2,384]{2,1,0:T(2,128)(2,1)S(1)}, u32[]{:S(2)}, u32[]{:S(2)}) %all-to-all-start) | async-done | bytes 196640 | tf_op jit(solution)/shard_map/all_to_all | solution.py:690
  22.2 0.7 reshape.17.args_1_.args_9_
  23.0 94.2 %first_step.1 = (bf16[2304,256]{1,0:T(8,128)(2,1)}, bf16[2304,256]{1,0:T(8,128)(2,1)}, bf16[27,512,256]{2,1,0:T(8,128)(2,1)}, s32[24,2304]{1,0:T(8,128)}, f32[23...) custom-call(bf16[2048,256]{1,0:T(8,128)(2,1)} %args_0_.4, bf16[256,384]{1,0:T(8,128)(2,1)} %reshape.17.args_1_.args_9_, ...), custom_call_target="tpu_custom_call" | custom-call | tf_op jit(solution)/shard_map/first_step/pallas_call | solution.py:510
  117.2 61.7 %last_step.1 = bf16[2304,256]{1,0:T(8,128)(2,1)} custom-call(s32[24,2304]{1,0:T(8,128)} %get-tuple-element.12.args_0_, f32[2304,128]{1,0:T(8,128)} %get-tuple-element.13.args_1_, bf16[2304,256]{1,0:T(8,128)(2,1)} %get-tuple-element.14.args_2_, bf16[2304,256]{1,0:T(8,128)(2,1)} %get-tuple-element.15.args_3_, bf16[27,512,256]{2,1,0:T(8,128)(2,1)} %get-tuple-element.16.args_4_, ...), custom_call_target="tpu_custom_call" | custom-call | tf_op jit(solution)/shard_map/last_step/pallas_call | solution.py:620
  (3 shorter events, 0.0 us)
Async XLA Ops:
  0.0 15.2 %copy-start = (s32[2304,24]{0,1:T(8,128)S(1)}, s32[2304,24]{0,1:T(8,128)}, u32[]{:S(2)}) copy-start(s32[2304,24]{0,1:T(8,128)} %param.21) | copy-start | bytes 663556
  4.1 18.1 %all-to-all-start = ((bf16[128,2,384]{2,1,0:T(2,128)(2,1)}), bf16[128,2,384]{2,1,0:T(2,128)(2,1)S(1)}, u32[]{:S(2)}, u32[]{:S(2)}) async-start(bf16[128,2,384]{2,1,0:T(2,128)(2,1)} %reshape.16), calls=%async_computation | async-start | bytes 393216 | tf_op jit(solution)/shard_map/all_to_all | solution.py:690

commit v5 on v4

--- a/solution.py
+++ b/solution.py
@@ -174,9 +174,11 @@
 
 
 CENTRE = (0, 0, 0)
-MIDDLE = [(dx, 0, 0) for dx in (-1, 1)]
-SIDES = [(dx, dy, 0) for dx in (0, -1, 1) for dy in (-1, 1)]
-ENDS = [(dx, dy, dz) for dx in (0, -1, 1) for dy in (0, -1, 1) for dz in (-1, 1)]
+OFFSETS = [(dx, dy, dz) for dx in (-1, 0, 1) for dy in (-1, 0, 1) for dz in (-1, 0, 1)]
+ALONG = [o for o in OFFSETS if o[:2] == (0, 0) and o[2] != 0]
+FACES = [o for o in OFFSETS if o[2] == 0 and abs(o[0]) + abs(o[1]) == 1]
+CORNERS = [o for o in OFFSETS if o[2] == 0 and o[0] != 0 and o[1] != 0]
+ENDS = [o for o in OFFSETS if o[2] != 0 and o[:2] != (0, 0)]
 
 
 class Exchange:
@@ -195,40 +197,67 @@
             device_id_type=MESH,
         )
 
-    def first_axis(self, offset):
-        return 0 if offset == CENTRE else 1 if offset in MIDDLE else 2
+    def on_chip(self, step):
+        return lax.rem(self.grid.place[2], 2) == (0 if step == 1 else 1)
+
+    def last_hops(self, offset):
+        dx, dy, dz = offset
+        if dz == 0:
+            if dx != 0 and dy != 0:
+                return [(1 if dx == dy else 0, None)]
+            return [(0 if dx != 0 else 1, None)]
+        if (dx != 0) == (dy != 0):
+            return [(2, None)]
+        near = self.on_chip(dz)
+        return [(2, near), (0 if dx != 0 else 1, jnp.logical_not(near))]
+
+    def hops_from(self, offset):
+        found = []
+        for axis in range(3):
+            if offset[axis] != 0:
+                continue
+            for step in (-1, 1):
+                dx, dy, dz = reached = moved(offset, axis, -step)
+                there = self.grid.inside(axis, step)
+                if offset != CENTRE:
+                    there = jnp.logical_and(there, self.grid.present(offset))
+                if dz != 0 and (dx != 0) != (dy != 0):
+                    near = self.on_chip(step if axis == 2 else dz)
+                    there = jnp.logical_and(there, near if axis == 2 else jnp.logical_not(near))
+                elif axis not in [a for a, _ in self.last_hops(reached)]:
+                    continue
+                found.append((axis, step, there))
+        return found
 
     def forward(self, offset):
-        for axis in range(self.first_axis(offset), 3):
-            for step in (-1, 1):
-
-                @pl.when(self.grid.inside(axis, step))
-                def _():
-                    self.copy(offset, axis, step).start()
+        for axis, step, there in self.hops_from(offset):
+
+            @pl.when(there)
+            def _():
+                self.copy(offset, axis, step).start()
 
     def arrive(self, offset):
-        axis = max(a for a in range(3) if offset[a] != 0)
-        self.copy(moved(offset, axis, -offset[axis]), axis, -offset[axis]).wait_recv()
+        for axis, condition in self.last_hops(offset):
+            there = self.grid.present(offset)
+            if condition is not None:
+                there = jnp.logical_and(there, condition)
+
+            @pl.when(there)
+            def _():
+                self.copy(moved(offset, axis, -offset[axis]), axis, -offset[axis]).wait_recv()
 
     def relay(self, offsets):
         for offset in offsets:
-
-            @pl.when(self.grid.present(offset))
-            def _():
-                self.arrive(offset)
-                self.forward(offset)
+            self.arrive(offset)
+            self.forward(offset)
 
     def finish_sends(self):
-        for offset in [CENTRE] + MIDDLE + SIDES:
-            for axis in range(self.first_axis(offset), 3):
-                for step in (-1, 1):
-                    there = self.grid.inside(axis, step)
-                    if offset != CENTRE:
-                        there = jnp.logical_and(there, self.grid.present(offset))
-
-                    @pl.when(there)
-                    def _():
-                        self.copy(offset, axis, step).wait_send()
+        for offset in [CENTRE] + ALONG + FACES + CORNERS:
+            for axis, step, there in self.hops_from(offset):
+
+                @pl.when(there)
+                def _():
+                    self.copy(offset, axis, step).wait_send()
 
 
 class EdgeLayers:
@@ -400,20 +429,23 @@
     layers = EdgeLayers(rows, slots, refs, scratch)
     grid.greet()
 
-    def take(first, values):
-        store_split(original, first, values.astype(F32))
-        store_split(pairs, first, project(values, send_weight[...]).astype(F32))
-
-    @pl.loop(0, local_rows // NODE_ROWS)
-    def _(i):
-        first = pl.multiple_of(i * NODE_ROWS, NODE_ROWS)
-        take(first, latent_ref[pl.ds(first, NODE_ROWS), :])
-
-    for first in range(0, arrivals, NODE_ROWS):
-        take(local_rows + first, arrived_ref[pl.ds(first, NODE_ROWS), :width])
-    copy_rows(pairs, halo_ids, ordered, boundary_rows)
-    boundary_ref[...] = load_split(ordered, 0, boundary_rows).astype(BF16)
+    def sources(take):
+        @pl.loop(0, local_rows // NODE_ROWS)
+        def _(i):
+            first = pl.multiple_of(i * NODE_ROWS, NODE_ROWS)
+            take(first, latent_ref[pl.ds(first, NODE_ROWS), :])
+
+        for first in range(0, arrivals, NODE_ROWS):
+            take(local_rows + first, arrived_ref[pl.ds(first, NODE_ROWS), :width])
+
+    sources(lambda first, values: store_split(original, first, values.astype(F32)))
+    copy_rows(original, halo_ids, ordered, boundary_rows)
+    for first in range(0, boundary_rows, NODE_ROWS):
+        values = load_split(ordered, first, NODE_ROWS).astype(BF16)
+        boundary_ref[pl.ds(first, NODE_ROWS), :] = project(values, send_weight[...])
     now.forward(CENTRE)
+    sources(lambda first, values: store_split(pairs, first, project(values, send_weight[...]).astype(F32)))
+    now.relay(ALONG)
     find_places(digits, halo_lanes, places, place_ref, count_ref)
 
     def spread(offset):
@@ -426,16 +458,15 @@
             def _():
                 spread(offset)
 
-    now.relay(MIDDLE)
-    now.relay(SIDES[:2])
+    now.relay(FACES)
     apply_places(pairs.shape[0] // 2, digits, places, edge_lanes, floor_ref, order_lanes)
     fetch_edges = pltpu.make_async_copy(edge_lanes, edge_ids, id_sems.at[0])
     fetch_order = pltpu.make_async_copy(order_lanes, order_ids, id_sems.at[1])
     fetch_edges.start()
     fetch_order.start()
-    spread_all(MIDDLE)
-    spread_all(SIDES[:2])
-    now.relay(SIDES[2:])
+    now.relay(CORNERS)
+    spread_all(ALONG)
+    spread_all(FACES)
     fetch_edges.wait()
     fetch_order.wait()
     copy_rows(original, order_ids.at[0], ordered, rows)
@@ -446,13 +477,10 @@
         table_ref[pl.ds(first, NODE_ROWS), :] = load_split(ordered, first, NODE_ROWS).astype(BF16)
 
     layers.prepare(table_ref)
-    spread_all(SIDES[2:])
+    spread_all(CORNERS)
     for offset in ENDS:
-
-        @pl.when(grid.present(offset))
-        def _():
-            now.arrive(offset)
-            spread(offset)
+        now.arrive(offset)
+        spread_all([offset])
 
     layers.gather(layers.buffers[0], 0, 0, layers.edges)
 
@@ -472,7 +500,7 @@
                 next_boundary[pl.ds(first, NODE_ROWS), :] = renew(first)
             later.forward(CENTRE)
 
-        for mark, offsets in zip(marks[1:], (MIDDLE, SIDES[:2], SIDES[2:])):
+        for mark, offsets in zip(marks[1:], (ALONG, FACES, CORNERS)):
 
             @pl.when(pair == mark)
             def _():
@@ -490,10 +518,7 @@
         renew(pl.multiple_of(i * NODE_ROWS, NODE_ROWS))
 
     for offset in ENDS:
-
-        @pl.when(grid.present(offset))
-        def _():
-            later.arrive(offset)
+        later.arrive(offset)
 
     now.finish_sends()
     later.finish_sends()
@@ -506,7 +531,7 @@
     count = halo_rows.shape[0]
     first_pair = count // ROWS // 2
     rest = blocks // 2 - first_pair
-    marks = (first_pair, first_pair + rest * 5 // 26, first_pair + rest * 7 // 26, first_pair + rest * 14 // 26)
+    marks = (first_pair, first_pair + rest * 4 // 26, first_pair + rest * 6 // 26, first_pair + rest * 10 // 26)
     return pl.pallas_call(
         functools.partial(first_step_kernel, slots, blocks, marks),
         out_shape=(

time: 179 us -> 178 us (level)
  the two profiles are of different devices: /device:TPU:18 before, /device:TPU:59 now
where the time goes in v5:
time: 178 us
  Pallas kernels  156 us (88%)
  starting transfers between devices  10.4 us (6%)
  waiting for transfers between devices  4.51 us (3%)
  other arithmetic  2.67 us (2%)
  matrix products  1.79 us (1%)
    pallas_call x1, Pallas kernels, first_step(): pl.pallas_call(functools.partial(first_step_kernel, slots, blocks, marks)...  95 us
    pallas_call x1, Pallas kernels, last_step(): pl.pallas_call(functools.partial(last_step_kernel, slots), out_shape=jax....  61 us
    all_to_all x1, starting transfers between devices, local(): lax.all_to_all(outgoing.reshape(devices, capacity, width + HALF), axes, s...  10.4 us
    all_to_all x1, waiting for transfers between devices, local(): lax.all_to_all(outgoing.reshape(devices, capacity, width + HALF), axes, s...  4.51 us
  transfers between devices with their start and end apart: 1, of which 1 were waited for; matrix products, arithmetic and copies ran while one was open for 1% of the time, Pallas kernels for 0%

profile of v5, /device:TPU:59, one launch (start us, length us, event | category | flops | bytes accessed | tf_op | source)
XLA Modules:
  0.0 177.7 jit_solution(16026416215296315902)
XLA Ops:
  0.0 0.0 copy-start
  0.0 0.9 convert_reduce_fusion
  0.9 0.7 multiply_add_fusion
  1.6 1.6 convolution_convert_fusion.1
  3.2 0.2 convolution_convert_fusion
  3.4 0.7 reshape.16
  4.1 10.4 %all-to-all-start = ((bf16[128,2,384]{2,1,0:T(2,128)(2,1)}), bf16[128,2,384]{2,1,0:T(2,128)(2,1)S(1)}, u32[]{:S(2)}, u32[]{:S(2)}) async-start(bf16[128,2,384]{2,1,0:T(2,128)(2,1)} %reshape.16), calls=%async_computation | async-start | bytes 393216 | tf_op jit(solution)/shard_map/all_to_all | solution.py:715
  15.2 0.1 pad.5.clone
  15.2 0.0 copy-done
  15.3 0.4 fusion.1
  15.6 0.7 pad_maximum_fusion.args_2_
  16.4 4.5 %all-to-all-done = bf16[128,2,384]{2,1,0:T(2,128)(2,1)S(1)} async-done(((bf16[128,2,384]{2,1,0:T(2,128)(2,1)}), bf16[128,2,384]{2,1,0:T(2,128)(2,1)S(1)}, u32[]{:S(2)}, u32[]{:S(2)}) %all-to-all-start) | async-done | bytes 196640 | tf_op jit(solution)/shard_map/all_to_all | solution.py:715
  20.9 0.7 reshape.17.args_1_.args_9_
  21.6 95.0 %first_step.1 = (bf16[2304,256]{1,0:T(8,128)(2,1)}, bf16[2304,256]{1,0:T(8,128)(2,1)}, bf16[27,512,256]{2,1,0:T(8,128)(2,1)}, s32[24,2304]{1,0:T(8,128)}, f32[23...) custom-call(bf16[2048,256]{1,0:T(8,128)(2,1)} %args_0_.4, bf16[256,384]{1,0:T(8,128)(2,1)} %reshape.17.args_1_.args_9_, ...), custom_call_target="tpu_custom_call" | custom-call | tf_op jit(solution)/shard_map/first_step/pallas_call | solution.py:535
  116.6 61.0 %last_step.1 = bf16[2304,256]{1,0:T(8,128)(2,1)} custom-call(s32[24,2304]{1,0:T(8,128)} %get-tuple-element.12.args_0_, f32[2304,128]{1,0:T(8,128)} %get-tuple-element.13.args_1_, bf16[2304,256]{1,0:T(8,128)(2,1)} %get-tuple-element.14.args_2_, bf16[2304,256]{1,0:T(8,128)(2,1)} %get-tuple-element.15.args_3_, bf16[27,512,256]{2,1,0:T(8,128)(2,1)} %get-tuple-element.16.args_4_, ...), custom_call_target="tpu_custom_call" | custom-call | tf_op jit(solution)/shard_map/last_step/pallas_call | solution.py:645
  (3 shorter events, 0.0 us)
Async XLA Ops:
  0.0 15.2 %copy-start = (s32[2304,24]{0,1:T(8,128)S(1)}, s32[2304,24]{0,1:T(8,128)}, u32[]{:S(2)}) copy-start(s32[2304,24]{0,1:T(8,128)} %param.21) | copy-start | bytes 663556
  4.1 16.8 %all-to-all-start = ((bf16[128,2,384]{2,1,0:T(2,128)(2,1)}), bf16[128,2,384]{2,1,0:T(2,128)(2,1)S(1)}, u32[]{:S(2)}, u32[]{:S(2)}) async-start(bf16[128,2,384]{2,1,0:T(2,128)(2,1)} %reshape.16), calls=%async_computation | async-start | bytes 393216 | tf_op jit(solution)/shard_map/all_to_all | solution.py:715

commit v6 on v5

--- a/solution.py
+++ b/solution.py
@@ -23,6 +23,13 @@
 VMEM = pl.BlockSpec(memory_space=pltpu.VMEM)
 SMEM = pl.BlockSpec(memory_space=pltpu.SMEM)
 ANYWHERE = pl.BlockSpec(memory_space=pl.ANY)
+
+
+def even_part(count, most=1024):
+    parts = -(-count // most)
+    while count % (parts * HALF):
+        parts += 1
+    return count // parts
 
 
 def layer_norm(values, feature_gain):
@@ -93,7 +100,7 @@
         place_ref[:, here] = jnp.transpose(place)[:1].astype(jnp.int32)
         return used + jnp.sum(others[:, :1]), spare + jnp.sum(idle[:, :1])
 
-    used, _ = lax.fori_loop(0, rows // n, one_chunk, (jnp.float32(0.0), jnp.float32(0.0)))
+    used, _ = lax.fori_loop(0, rows // n, one_chunk, (jnp.float32(0.0), jnp.float32(0.0)), unroll=3)
     count_ref[0] = used.astype(jnp.int32) + boundary
 
 
@@ -103,7 +110,7 @@
     slots = half_rows - SPARE
     n = NODE_ROWS
 
-    @pl.loop(0, rows // n)
+    @pl.loop(0, rows // n, unroll=3)
     def _(c):
         first = pl.multiple_of(c * n, n)
         lanes = lax.broadcasted_iota(jnp.int32, (n, HALF), 1).astype(F32)
@@ -274,7 +281,7 @@
         wide = refs["edge_out"][...].astype(F32)
         self.weight[...] = (wide - jnp.mean(wide, axis=1, keepdims=True)).astype(BF16)
 
-        @pl.loop(0, self.rows // NODE_ROWS)
+        @pl.loop(0, self.rows // NODE_ROWS, unroll=3)
         def _(i):
             here = pl.ds(pl.multiple_of(i * NODE_ROWS, NODE_ROWS), NODE_ROWS)
             self.summed[here, :] = jnp.zeros((NODE_ROWS, self.width), F32)
@@ -484,8 +491,8 @@
 
     layers.gather(layers.buffers[0], 0, 0, layers.edges)
 
-    def renew(first):
-        here = pl.ds(first, NODE_ROWS)
+    def renew(first, count):
+        here = pl.ds(first, count)
         renewed = node_layers(refs, table_ref, summed, here).astype(BF16)
         renewed_ref[here, :] = renewed
         projected = project(renewed, next_weight[...])
@@ -496,8 +503,7 @@
     def _(pair):
         @pl.when(pair == marks[0])
         def _():
-            for first in range(0, boundary_rows, NODE_ROWS):
-                next_boundary[pl.ds(first, NODE_ROWS), :] = renew(first)
+            next_boundary[...] = renew(0, boundary_rows)
             later.forward(CENTRE)
 
         for mark, offsets in zip(marks[1:], (ALONG, FACES, CORNERS)):
@@ -513,9 +519,11 @@
             def _():
                 layers.one_block(block, parity, blocks - 1)
 
-    @pl.loop(boundary_rows // NODE_ROWS, rows // NODE_ROWS)
+    part = even_part(rows - boundary_rows)
+
+    @pl.loop(0, (rows - boundary_rows) // part)
     def _(i):
-        renew(pl.multiple_of(i * NODE_ROWS, NODE_ROWS))
+        renew(pl.multiple_of(boundary_rows + i * part, HALF), part)
 
     for offset in ENDS:
         later.arrive(offset)
@@ -616,10 +624,12 @@
             def _():
                 layers.one_block(block, parity, rows // ROWS - 1)
 
-    @pl.loop(0, rows // NODE_ROWS)
+    part = even_part(rows)
+
+    @pl.loop(0, rows // part)
     def _(i):
-        first = pl.multiple_of(i * NODE_ROWS, NODE_ROWS)
-        renewed = node_layers(refs, table_ref, summed, pl.ds(first, NODE_ROWS))
+        first = pl.multiple_of(i * part, HALF)
+        renewed = node_layers(refs, table_ref, summed, pl.ds(first, part))
         store_split(ordered, first, renewed)
 
     copy_rows(ordered, place_ids.at[0], pairs, rows)

time: 178 us -> 172 us (0.966)
  the two profiles are of different devices: /device:TPU:59 before, /device:TPU:58 now
where the time goes in v6:
time: 172 us; the launch traced here: 171 us
  Pallas kernels  150 us (87%)
  starting transfers between devices  10.1 us (6%)
  waiting for transfers between devices  4.57 us (3%)
  other arithmetic  2.67 us (2%)
  matrix products  1.79 us (1%)
    pallas_call x1, Pallas kernels, first_step(): pl.pallas_call(functools.partial(first_step_kernel, slots, blocks, marks)...  92.4 us
    pallas_call x1, Pallas kernels, last_step(): pl.pallas_call(functools.partial(last_step_kernel, slots), out_shape=jax....  57.5 us
    all_to_all x1, starting transfers between devices, local(): lax.all_to_all(outgoing.reshape(devices, capacity, width + HALF), axes, s...  10.1 us
    all_to_all x1, waiting for transfers between devices, local(): lax.all_to_all(outgoing.reshape(devices, capacity, width + HALF), axes, s...  4.57 us
  transfers between devices with their start and end apart: 1, of which 1 were waited for; matrix products, arithmetic and copies ran while one was open for 1% of the time, Pallas kernels for 0%

profile of v6, /device:TPU:58, one launch (start us, length us, event | category | flops | bytes accessed | tf_op | source)
XLA Modules:
  0.0 171.3 jit_solution(8828753103711857851)
XLA Ops:
  0.0 0.0 copy-start
  0.0 0.9 convert_reduce_fusion
  0.9 0.7 multiply_add_fusion
  1.6 1.6 convolution_convert_fusion.1
  3.2 0.2 convolution_convert_fusion
  3.4 0.7 reshape.16
  4.1 10.1 %all-to-all-start = ((bf16[128,2,384]{2,1,0:T(2,128)(2,1)}), bf16[128,2,384]{2,1,0:T(2,128)(2,1)S(1)}, u32[]{:S(2)}, u32[]{:S(2)}) async-start(bf16[128,2,384]{2,1,0:T(2,128)(2,1)} %reshape.16), calls=%async_computation | async-start | bytes 393216 | tf_op jit(solution)/shard_map/all_to_all | solution.py:725
  14.8 0.1 pad.5.clone
  14.9 0.0 copy-done
  15.0 0.4 fusion.1
  15.3 0.7 pad_maximum_fusion.args_2_
  16.1 4.6 %all-to-all-done = bf16[128,2,384]{2,1,0:T(2,128)(2,1)S(1)} async-done(((bf16[128,2,384]{2,1,0:T(2,128)(2,1)}), bf16[128,2,384]{2,1,0:T(2,128)(2,1)S(1)}, u32[]{:S(2)}, u32[]{:S(2)}) %all-to-all-start) | async-done | bytes 196640 | tf_op jit(solution)/shard_map/all_to_all | solution.py:725
  20.6 0.7 reshape.17.args_1_.args_9_
  21.4 92.4 %first_step.1 = (bf16[2304,256]{1,0:T(8,128)(2,1)}, bf16[2304,256]{1,0:T(8,128)(2,1)}, bf16[27,512,256]{2,1,0:T(8,128)(2,1)}, s32[24,2304]{1,0:T(8,128)}, f32[23...) custom-call(bf16[2048,256]{1,0:T(8,128)(2,1)} %args_0_.4, bf16[256,384]{1,0:T(8,128)(2,1)} %reshape.17.args_1_.args_9_, ...), custom_call_target="tpu_custom_call" | custom-call | tf_op jit(solution)/shard_map/first_step/pallas_call | solution.py:543
  113.8 57.5 %last_step.1 = bf16[2304,256]{1,0:T(8,128)(2,1)} custom-call(s32[24,2304]{1,0:T(8,128)} %get-tuple-element.12.args_0_, f32[2304,128]{1,0:T(8,128)} %get-tuple-element.13.args_1_, bf16[2304,256]{1,0:T(8,128)(2,1)} %get-tuple-element.14.args_2_, bf16[2304,256]{1,0:T(8,128)(2,1)} %get-tuple-element.15.args_3_, bf16[27,512,256]{2,1,0:T(8,128)(2,1)} %get-tuple-element.16.args_4_, ...), custom_call_target="tpu_custom_call" | custom-call | tf_op jit(solution)/shard_map/last_step/pallas_call | solution.py:655
  (3 shorter events, 0.0 us)
Async XLA Ops:
  0.0 14.9 %copy-start = (s32[2304,24]{0,1:T(8,128)S(1)}, s32[2304,24]{0,1:T(8,128)}, u32[]{:S(2)}) copy-start(s32[2304,24]{0,1:T(8,128)} %param.21) | copy-start | bytes 663556
  4.1 16.5 %all-to-all-start = ((bf16[128,2,384]{2,1,0:T(2,128)(2,1)}), bf16[128,2,384]{2,1,0:T(2,128)(2,1)S(1)}, u32[]{:S(2)}, u32[]{:S(2)}) async-start(bf16[128,2,384]{2,1,0:T(2,128)(2,1)} %reshape.16), calls=%async_computation | async-start | bytes 393216 | tf_op jit(solution)/shard_map/all_to_all | solution.py:725
